TPU v7x, 128 devices: a whole 4x4x4 slice. The times are simulated.
128 devices in a mesh: shot: 8 (over x, core), sub: 16 (over z, y).
Axes of the slice: x: 4, y: 4, z: 4, core: 2. Of those that a mesh axis runs over, the one named last changes fastest.
Arguments:
- wave_now: float32 [8, 256, 128, 256], P('shot', 'sub'), may hold values from -6 to 6
- wave_before: float32 [8, 256, 128, 256], P('shot', 'sub'), may hold values from -6 to 6
- courant: float32 [8, 256, 128, 256], P('shot', 'sub'), may hold values from 0.05 to 0.2
- source_waves: bfloat16 [4, 8, 256, 128, 256], P(None, 'shot', 'sub'), may hold values from -6 to 6
- tile_ids: int32 [8, 8192, 1], P('shot', 'sub'), may hold values from 0 to 127; in each aligned block of 512 rows (0 to 511, 512 to 1023, ..., all dimensions but the last counted through in order) at most 8 rows name the same one
- slot_ids: int32 [8, 8192], P('shot', 'sub'), may hold values from 0 to 15
Outputs:
- wave_last: float32 [8, 256, 128, 256], P('shot', 'sub')
- wave_prior: float32 [8, 256, 128, 256], P('shot', 'sub')
- image: float32 [128, 16, 1024], P(('shot', 'sub'))
Inputs may be any that keep to these rules, and one draw needn't show every extreme that they name: `tile_ids`: among the 512 blocks of one device no tile is named more than 8 times, a bound that some block reaches; every tile is named somewhere.
All inputs are finite; a program needn't handle non-finite values.
Results may differ from a plain program's by a relative error of at most 0.0003.
Values sent between devices are 32-bit elements; how exact they have to be, the bound alone decides.
A program may use at most 128 MiB of HBM per device.

v0:
```python
import jax
import jax.numpy as jnp
from jax import lax
from jax.sharding import PartitionSpec as P

ITERS = 4
BY = 4
TSLOTS = 16


fd_weights = (-205.0 / 72.0, 8.0 / 5.0, -1.0 / 5.0, 8.0 / 315.0, -1.0 / 560.0)


def with_halo(cells, sides, width):
    for axis, dim in sides:
        count = lax.axis_size(axis)
        ends = count - 1
        head = lax.slice_in_dim(cells, 0, width, axis=dim)
        tail = lax.slice_in_dim(cells, cells.shape[dim] - width, cells.shape[dim], axis=dim)
        cells = jnp.concatenate(
            [
                lax.ppermute(tail, axis, [(i, (i + 1) % count) for i in range(ends)]),
                cells,
                lax.ppermute(head, axis, [((i + 1) % count, i) for i in range(ends)]),
            ],
            axis=dim,
        )
    return cells


def laplace(field):
    length = field.shape[-3]
    width_y = field.shape[-2]
    width_z = field.shape[-1]
    core = field[..., 4 : length - 4, :, :]
    padded = jnp.pad(core, [(0, 0)] * (core.ndim - 2) + [(4, 4), (4, 4)])
    total = 3.0 * fd_weights[0] * core
    for k in range(1, 5):
        total = total + fd_weights[k] * (
            field[..., 4 + k : length - 4 + k, :, :] + field[..., 4 - k : length - 4 - k, :, :]
        )
        total = total + fd_weights[k] * (
            padded[..., 4 + k : 4 + k + width_y, 4 : 4 + width_z]
            + padded[..., 4 - k : 4 - k + width_y, 4 : 4 + width_z]
        )
        total = total + fd_weights[k] * (
            padded[..., 4 : 4 + width_y, 4 + k : 4 + k + width_z]
            + padded[..., 4 : 4 + width_y, 4 - k : 4 - k + width_z]
        )
    return total


def on_device(wave_now, wave_before, courant, source_waves, tile_ids, slot_ids):
    cells_x = wave_now.shape[1]
    current = wave_now
    before = wave_before
    partial_value = jnp.zeros_like(wave_now)
    for step in range(ITERS):
        padded = with_halo(current, (("sub", 1),), 4)
        after = 2.0 * current - before + courant * laplace(padded)
        before = current
        current = after
        partial_value = partial_value + source_waves[step].astype(jnp.float32) * current
    num_blocks = cells_x * wave_now.shape[2] // BY
    block_size = BY * wave_now.shape[3]
    blocks = partial_value.reshape(num_blocks, block_size)
    tiles_here = tile_ids.reshape(num_blocks)
    slots_here = slot_ids.reshape(num_blocks)
    keys = tiles_here * TSLOTS + slots_here
    picker = (
        keys[:, None]
        == jnp.arange(TSLOTS * lax.axis_size(("shot", "sub")), dtype=jnp.int32)[None, :]
    ).astype(jnp.float32)
    image = lax.psum_scatter(
        jnp.dot(
            picker.T, blocks, precision=lax.Precision.HIGHEST, preferred_element_type=jnp.float32
        ),
        ("shot", "sub"),
        scatter_dimension=0,
        tiled=True,
    )
    return (current, before, image.reshape(1, TSLOTS, block_size))


def solution(mesh):
    return jax.shard_map(
        on_device,
        mesh=mesh,
        in_specs=(
            P("shot", "sub", None, None),
            P("shot", "sub", None, None),
            P("shot", "sub", None, None),
            P(None, "shot", "sub", None, None),
            P("shot", "sub", None),
            P("shot", "sub"),
        ),
        out_specs=(
            P("shot", "sub", None, None),
            P("shot", "sub", None, None),
            P(("shot", "sub"), None, None),
        ),
        check_vma=False,
    )
```

profile of v0, /device:TPU:0, one launch (start us, length us, event | category | flops | bytes accessed | tf_op | source)
XLA Modules:
  0.0 787.2 jit_solution(12219919624851411694)
XLA Ops:
  7.2 1.4 fusion.175
  8.6 3.6 collective-permute-start.1
  12.2 1.3 collective-permute-start
  13.5 9.8 %collective-permute-done.1 = f32[1,4,128,256]{3,2,1,0:T(8,128)S(1)} collective-permute-done((f32[1,4,128,256]{3,2,1,0:T(8,128)S(1)}, f32[1,4,128,256]{3,2,1,0:T(8,128)S(1)}, u32[]{:S(2)}, u32[]{:S(2)}) %collective-permute-start.1) | collective-permute-done | bytes 524320 | tf_op jit(solution)/shard_map/ppermute | solution.py:22
  23.9 3.6 collective-permute-done
  27.6 4.9 fusion.93
  32.5 1.3 collective-permute-start.2
  33.8 4.6 collective-permute-start.3
  38.4 8.5 %collective-permute-done.2 = f32[1,4,128,256]{3,2,1,0:T(8,128)S(1)} collective-permute-done((f32[1,4,128,256]{3,2,1,0:T(8,128)S(1)}, f32[1,4,128,256]{3,2,1,0:T(8,128)S(1)}, u32[]{:S(2)}, u32[]{:S(2)}) %collective-permute-start.2) | collective-permute-done | bytes 524320 | tf_op jit(solution)/shard_map/ppermute | solution.py:24
  46.9 1.2 collective-permute-done.3
  48.1 8.6 %fusion.63 = f32[1,16,128,256]{3,2,1,0:T(8,128)S(1)} fusion(f32[1,16,128,256]{3,2,1,0:T(8,128)S(1)} %copy-done, f32[1,16,128,256]{3,2,1,0:T(8,128)S(1)} %fusion.93, f32[1,4,128,256]{3,2,1,0:T(8,128)S(1)} %collective-permute-done.3, f32[1,4,128,256]{3,2,1,0:T(8,128)S(1)} %collective-permute-done.2, f32[1,16,128,256]{3,2,1,0:T(8,128)S(1)} %copy-done.1), kind=kLoop, calls=%fused_computation.164 | loop fusion | flops 25690112 | bytes 9437184 | tf_op jit(solution)/shard_map/add | solution.py:60
  56.8 1.3 collective-permute-start.4
  58.1 5.0 collective-permute-start.5
  63.1 7.6 collective-permute-done.4
  70.7 1.2 collective-permute-done.5
  71.9 8.6 %fusion.37 = f32[1,16,128,256]{3,2,1,0:T(8,128)S(1)} fusion(f32[1,16,128,256]{3,2,1,0:T(8,128)S(1)} %copy-done, f32[1,16,128,256]{3,2,1,0:T(8,128)S(1)} %fusion.63, f32[1,4,128,256]{3,2,1,0:T(8,128)S(1)} %collective-permute-done.5, f32[1,4,128,256]{3,2,1,0:T(8,128)S(1)} %collective-permute-done.4, f32[1,16,128,256]{3,2,1,0:T(8,128)S(1)} %fusion.93), kind=kLoop, calls=%fused_computation.138 | loop fusion | flops 25690112 | bytes 9437184 | tf_op jit(solution)/shard_map/add | solution.py:60
  80.6 1.3 collective-permute-start.6
  81.9 5.9 collective-permute-start.7
  87.8 6.2 collective-permute-done.6
  94.1 1.1 collective-permute-done.7
  95.1 11.8 %fusion.167 = (f32[1,16,128,256]{3,2,1,0:T(8,128)}, f32[1,16,128,256]{3,2,1,0:T(8,128)}) fusion(f32[1,16,128,256]{3,2,1,0:T(8,128)S(1)} %fusion.37, f32[1,16,128,256]{3,2,1,0:T(8,128)} %copy-done.2, f32[1,16,128,256]{3,2,1,0:T(8,128)S(1)} %fusion.93, bf16[4,1,16,128,256]{4,3,2,1,0:T(8,128)(2,1)} %param.9, f32[1,16,128,256]{3,2,1,0:T(8,128)S(1)} %copy-done, ...), kind=kLoop, calls=%fused_computation.279 | loop fusion | flops 31457280 | bytes 17825792 | tf_op jit(solution)/shard_map/add | solution.py:63
  106.9 1.9 reshape.85
  108.8 9.3 %fusion = f32[2048,1024]{1,0:T(8,128)} fusion(f32[512,1024]{1,0:T(8,128)S(1)} %reshape.85, s32[512]{0:T(512)S(1)} %add.426), kind=kOutput, calls=%fused_computation.83 | convolution fusion | flops 12885950464 | bytes 10487808 | tf_op jit(solution)/shard_map/dot_general | solution.py:75
  118.1 662.3 %reduce-scatter.2.cloned.1.call-done = f32[16,1024]{1,0:T(8,128)} async-done(((f32[2048,1024]{1,0:T(8,128)}), f32[16,1024]{1,0:T(8,128)}) %reduce-scatter.2.cloned.1.call-update) | async-done | bytes 65552 | tf_op jit(solution)/shard_map/reduce_scatter | solution.py:74
  (24 shorter events, 0.9 us)
Async XLA Ops:
  7.2 16.2 %copy-start.1 = (f32[1,16,128,256]{3,2,1,0:T(8,128)S(1)}, f32[1,16,128,256]{3,2,1,0:T(8,128)}, u32[]{:S(2)}) copy-start(f32[1,16,128,256]{3,2,1,0:T(8,128)} %param.6) | copy-start | bytes 6291460
  7.2 773.2 %reduce-scatter.2.cloned.1.call-start = ((), (), s32[]{:S(2)}) async-start(), calls=%async_computation.1 | async-start | bytes 8454144 | tf_op jit(solution)/shard_map/reduce_scatter | solution.py:74
  8.6 14.7 %collective-permute-start.1 = (f32[1,4,128,256]{3,2,1,0:T(8,128)S(1)}, f32[1,4,128,256]{3,2,1,0:T(8,128)S(1)}, u32[]{:S(2)}, u32[]{:S(2)}) collective-permute-start(f32[1,4,128,256]{3,2,1,0:T(8,128)S(1)} %get-tuple-element.12), channel_id=1, source_target_pairs={{0,1},{1,2},{2,3},{3,4},{4,5},{5,6},{6,7},{7,8},{8,9},{9,10},{10,1... | collective-permute-start | bytes 1572872 | tf_op jit(solution)/shard_map/ppermute | solution.py:22
  12.2 15.3 %collective-permute-start = (f32[1,4,128,256]{3,2,1,0:T(8,128)S(1)}, f32[1,4,128,256]{3,2,1,0:T(8,128)S(1)}, u32[]{:S(2)}, u32[]{:S(2)}) collective-permute-start(f32[1,4,128,256]{3,2,1,0:T(8,128)S(1)} %get-tuple-element.11), channel_id=1, source_target_pairs={{1,0},{2,1},{3,2},{4,3},{5,4},{6,5},{7,6},{8,7},{9,8},{10,9},{11,1... | collective-permute-start | bytes 1572872 | tf_op jit(solution)/shard_map/ppermute | solution.py:24
  23.4 4.1 copy-start
  23.4 4.1 copy-start.4
  32.5 14.4 %collective-permute-start.2 = (f32[1,4,128,256]{3,2,1,0:T(8,128)S(1)}, f32[1,4,128,256]{3,2,1,0:T(8,128)S(1)}, u32[]{:S(2)}, u32[]{:S(2)}) collective-permute-start(f32[1,4,128,256]{3,2,1,0:T(8,128)S(1)} %get-tuple-element.9), channel_id=1, source_target_pairs={{1,0},{2,1},{3,2},{4,3},{5,4},{6,5},{7,6},{8,7},{9,8},{10,9},{11,1... | collective-permute-start | bytes 1572872 | tf_op jit(solution)/shard_map/ppermute | solution.py:24
  33.8 14.2 %collective-permute-start.3 = (f32[1,4,128,256]{3,2,1,0:T(8,128)S(1)}, f32[1,4,128,256]{3,2,1,0:T(8,128)S(1)}, u32[]{:S(2)}, u32[]{:S(2)}) collective-permute-start(f32[1,4,128,256]{3,2,1,0:T(8,128)S(1)} %get-tuple-element.10), channel_id=1, source_target_pairs={{0,1},{1,2},{2,3},{3,4},{4,5},{5,6},{6,7},{7,8},{8,9},{9,10},{10,1... | collective-permute-start | bytes 1572872 | tf_op jit(solution)/shard_map/ppermute | solution.py:22
  56.7 23.9 %copy-start.2 = (f32[1,16,128,256]{3,2,1,0:T(8,128)}, f32[1,16,128,256]{3,2,1,0:T(8,128)S(1)}, u32[]{:S(2)}) copy-start(f32[1,16,128,256]{3,2,1,0:T(8,128)S(1)} %fusion.63) | copy-start | bytes 6291460
  56.8 13.9 %collective-permute-start.4 = (f32[1,4,128,256]{3,2,1,0:T(8,128)S(1)}, f32[1,4,128,256]{3,2,1,0:T(8,128)S(1)}, u32[]{:S(2)}, u32[]{:S(2)}) collective-permute-start(f32[1,4,128,256]{3,2,1,0:T(8,128)S(1)} %get-tuple-element.7), channel_id=1, source_target_pairs={{1,0},{2,1},{3,2},{4,3},{5,4},{6,5},{7,6},{8,7},{9,8},{10,9},{11,1... | collective-permute-start | bytes 1572872 | tf_op jit(solution)/shard_map/ppermute | solution.py:24
  58.1 13.8 %collective-permute-start.5 = (f32[1,4,128,256]{3,2,1,0:T(8,128)S(1)}, f32[1,4,128,256]{3,2,1,0:T(8,128)S(1)}, u32[]{:S(2)}, u32[]{:S(2)}) collective-permute-start(f32[1,4,128,256]{3,2,1,0:T(8,128)S(1)} %get-tuple-element.8), channel_id=1, source_target_pairs={{0,1},{1,2},{2,3},{3,4},{4,5},{5,6},{6,7},{7,8},{8,9},{9,10},{10,1... | collective-permute-start | bytes 1572872 | tf_op jit(solution)/shard_map/ppermute | solution.py:22
  80.4 26.4 %copy-start.3 = (f32[1,16,128,256]{3,2,1,0:T(8,128)}, f32[1,16,128,256]{3,2,1,0:T(8,128)S(1)}, u32[]{:S(2)}) copy-start(f32[1,16,128,256]{3,2,1,0:T(8,128)S(1)} %fusion.37) | copy-start | bytes 6291460
  80.5 7.3 copy-start.6
  80.5 7.3 copy-start.5
  80.6 13.5 %collective-permute-start.6 = (f32[1,4,128,256]{3,2,1,0:T(8,128)S(1)}, f32[1,4,128,256]{3,2,1,0:T(8,128)}, u32[]{:S(2)}, u32[]{:S(2)}) collective-permute-start(f32[1,4,128,256]{3,2,1,0:T(8,128)S(1)} %get-tuple-element.5), channel_id=1, source_target_pairs={{1,0},{2,1},{3,2},{4,3},{5,4},{6,5},{7,6},{8,7},{9,8},{10,9},{11,1... | collective-permute-start | bytes 1572872 | tf_op jit(solution)/shard_map/ppermute | solution.py:24
  81.9 13.3 %collective-permute-start.7 = (f32[1,4,128,256]{3,2,1,0:T(8,128)S(1)}, f32[1,4,128,256]{3,2,1,0:T(8,128)}, u32[]{:S(2)}, u32[]{:S(2)}) collective-permute-start(f32[1,4,128,256]{3,2,1,0:T(8,128)S(1)} %get-tuple-element.6), channel_id=1, source_target_pairs={{0,1},{1,2},{2,3},{3,4},{4,5},{5,6},{6,7},{7,8},{8,9},{9,10},{10,1... | collective-permute-start | bytes 1572872 | tf_op jit(solution)/shard_map/ppermute | solution.py:22
Sparse Core Ops, SparseCore 0:
  118.2 662.1 reduce-scatter.1
where the time goes:
time: 788 us; the launch traced here: 787 us
  waiting for transfers between devices  701 us (89%)
  other arithmetic  33.8 us (4%)
  starting transfers between devices  24.3 us (3%)
  between operations  14.3 us (2%)
  matrix products  9.3 us (1%)
    reduce_scatter x1, waiting for transfers between devices, on_device(): lax.psum_scatter(jnp.dot(picker.T, blocks, precision=lax.Precision.HIGHES...  662 us
    ppermute x4, waiting for transfers between devices, with_halo(): lax.ppermute(head, axis, [((i + 1) % count, i) for i in range(ends)])  25.9 us
    add x3, other arithmetic, on_device(): after = 2.0 * current - before + courant * laplace(padded)  22 us
    ppermute x4, starting transfers between devices, with_halo(): lax.ppermute(tail, axis, [(i, (i + 1) % count) for i in range(ends)])  19.1 us
  transfers between devices with their start and end apart: 9, of which 9 were waited for; matrix products, arithmetic and copies ran while one was open for 0% of the time, Pallas kernels for 0%

commit v1 on v0

v1 whole, which is shorter than its diff:
```python
import jax
import jax.numpy as jnp
from jax import lax
from jax.experimental import pallas as pl
from jax.experimental.pallas import tpu as pltpu
from jax.sharding import PartitionSpec as P

ITERS = 4
BY = 4
TSLOTS = 16
MESH = pl.DeviceIdType.MESH
W = (-205.0 / 72.0, 8.0 / 5.0, -1.0 / 5.0, 8.0 / 315.0, -1.0 / 560.0)

NX, CY, CZ = 16, 128, 256
ROWS = 16
CHUNKS = CY // ROWS
PAD = 8
MIB = 1024 * 1024


def bf(v):
    return v.astype(jnp.bfloat16)


def f32(v):
    return v.astype(jnp.float32)


def steps_kernel(now, before, courant, source, last, prior, image, wave, speed, src, part, zpart, band, load, send, recv, store):
    sub = lax.axis_index("sub")
    count = lax.axis_size("sub")
    has_left = sub > 0
    has_right = sub < count - 1
    left = {"sub": jnp.maximum(sub - 1, 0)}
    right = {"sub": jnp.minimum(sub + 1, count - 1)}

    inner = (pl.ds(4, NX), pl.ds(PAD, CY))
    loads = [
        pltpu.make_async_copy(now.at[0], wave.at[(0, *inner)], load.at[0]),
        pltpu.make_async_copy(before.at[0], wave.at[(1, *inner)], load.at[1]),
        pltpu.make_async_copy(courant.at[0], speed, load.at[2]),
    ]
    loads += [pltpu.make_async_copy(source.at[t, 0], src.at[t], load.at[3 + t]) for t in range(ITERS)]
    for copy in loads:
        copy.start()

    barrier = pltpu.get_barrier_semaphore()

    @pl.when(has_left)
    def _():
        pl.semaphore_signal(barrier, inc=1, device_id=left, device_id_type=MESH)

    @pl.when(has_right)
    def _():
        pl.semaphore_signal(barrier, inc=1, device_id=right, device_id_type=MESH)

    edge = jnp.zeros((2, 4, CY, CZ), jnp.float32)

    @pl.when(jnp.logical_not(has_left))
    def _():
        wave[:, 0:4, PAD : PAD + CY, :] = edge

    @pl.when(jnp.logical_not(has_right))
    def _():
        wave[:, NX + 4 : NX + 8, PAD : PAD + CY, :] = edge

    strip = jnp.zeros((2, NX, PAD, CZ), jnp.float32)
    wave[:, 4 : NX + 4, 0:PAD, :] = strip
    wave[:, 4 : NX + 4, PAD + CY :, :] = strip
    gap = jnp.abs(lax.broadcasted_iota(jnp.int32, (CZ, CZ), 0) - lax.broadcasted_iota(jnp.int32, (CZ, CZ), 1))
    taps = jnp.zeros((CZ, CZ), jnp.float32)
    for k in range(1, 5):
        taps = jnp.where(gap == k, W[k], taps)
    band[0] = bf(taps)
    band[1] = bf(taps - f32(bf(taps)))

    pl.semaphore_wait(barrier, jnp.where(has_left, 1, 0) + jnp.where(has_right, 1, 0))

    def to_left(t, j, source_ref=None):
        b = lax.rem(t, 2)
        rows = pl.ds(PAD + j * ROWS, ROWS)
        return pltpu.make_async_remote_copy(
            src_ref=source_ref if source_ref is not None else wave.at[b, pl.ds(4, 4), rows],
            dst_ref=wave.at[b, pl.ds(NX + 4, 4), rows],
            send_sem=send.at[0, t, j],
            recv_sem=recv.at[0, t, j],
            device_id=left,
            device_id_type=MESH,
        )

    def to_right(t, j, source_ref=None):
        b = lax.rem(t, 2)
        rows = pl.ds(PAD + j * ROWS, ROWS)
        return pltpu.make_async_remote_copy(
            src_ref=source_ref if source_ref is not None else wave.at[b, pl.ds(NX, 4), rows],
            dst_ref=wave.at[b, pl.ds(0, 4), rows],
            send_sem=send.at[1, t, j],
            recv_sem=recv.at[1, t, j],
            device_id=right,
            device_id_type=MESH,
        )

    def first(j, _):
        rows = pl.ds(j * ROWS, ROWS)

        @pl.when(has_left)
        def _():
            to_left(0, j, now.at[0, pl.ds(0, 4), rows]).start()

        @pl.when(has_right)
        def _():
            to_right(0, j, now.at[0, pl.ds(NX - 4, 4), rows]).start()

        return 0

    lax.fori_loop(0, CHUNKS, first, 0)

    for copy in loads[:3]:
        copy.wait()

    def chunk(t, j):
        cur = lax.rem(t, 2)
        nxt = 1 - cur
        row0 = j * ROWS
        rows = pl.ds(pl.multiple_of(PAD + row0, 8), ROWS)
        plain = pl.ds(pl.multiple_of(row0, ROWS), ROWS)

        v = wave[cur, pl.ds(4, NX), rows, :].reshape(NX * ROWS, CZ)
        hi = bf(v)
        lo = bf(v - f32(hi))
        z = jnp.dot(hi, band[0], preferred_element_type=jnp.float32)
        z += jnp.dot(lo, band[0], preferred_element_type=jnp.float32)
        z += jnp.dot(hi, band[1], preferred_element_type=jnp.float32)
        zpart[...] = z.reshape(NX, ROWS, CZ)

        @pl.when(has_left)
        def _():
            to_right(t, j).wait_recv()

            @pl.when(t > 0)
            def _():
                to_left(t, j).wait_send()

        @pl.when(has_right)
        def _():
            to_left(t, j).wait_recv()

            @pl.when(t > 0)
            def _():
                to_right(t, j).wait_send()

        def layer(x, _):
            wide = wave[cur, x + 4, pl.ds(pl.multiple_of(row0, 8), ROWS + 2 * PAD), :]
            center = wide[PAD : PAD + ROWS]
            lap = 3.0 * W[0] * center + zpart[x]
            for k in range(1, 5):
                pair = wave[cur, x + 4 + k, rows, :] + wave[cur, x + 4 - k, rows, :]
                pair += wide[PAD + k : PAD + k + ROWS] + wide[PAD - k : PAD - k + ROWS]
                lap += W[k] * pair
            after = 2.0 * center - wave[nxt, x + 4, rows, :] + speed[x, plain, :] * lap
            wave[nxt, x + 4, rows, :] = after
            term = f32(src[t, x, plain, :]) * after
            part[x, plain, :] = jnp.where(t == 0, term, part[x, plain, :] + term)
            return 0

        lax.fori_loop(0, NX, layer, 0)

        @pl.when(t < ITERS - 1)
        def _():
            @pl.when(has_left)
            def _():
                to_left(t + 1, j).start()

            @pl.when(has_right)
            def _():
                to_right(t + 1, j).start()

    def last_copies(j):
        rows = pl.ds(pl.multiple_of(PAD + j * ROWS, 8), ROWS)
        plain = pl.ds(pl.multiple_of(j * ROWS, ROWS), ROWS)
        final = ITERS % 2
        return (
            pltpu.make_async_copy(wave.at[final, pl.ds(4, NX), rows], last.at[0, :, plain], store.at[0, j]),
            pltpu.make_async_copy(part.at[:, plain], image.at[:, plain], store.at[1, j]),
        )

    prior_copy = pltpu.make_async_copy(wave.at[((ITERS + 1) % 2, *inner)], prior.at[0], store.at[2, 0])

    def one_step(t, _):
        for s in range(ITERS):

            @pl.when(t == s)
            def _():
                loads[3 + s].wait()

        @pl.when(t == ITERS - 1)
        def _():
            prior_copy.start()

        def one_chunk(j, _):
            chunk(t, j)

            @pl.when(t == ITERS - 1)
            def _():
                for copy in last_copies(j):
                    copy.start()

            return 0

        lax.fori_loop(0, CHUNKS, one_chunk, 0)
        return 0

    lax.fori_loop(0, ITERS, one_step, 0)

    def finish(j, _):
        for copy in last_copies(j):
            copy.wait()
        rows = pl.ds(j * ROWS, ROWS)

        @pl.when(has_left)
        def _():
            to_left(0, j, now.at[0, pl.ds(0, 4), rows]).wait_send()

        @pl.when(has_right)
        def _():
            to_right(0, j, now.at[0, pl.ds(NX - 4, 4), rows]).wait_send()

        return 0

    lax.fori_loop(0, CHUNKS, finish, 0)
    prior_copy.wait()


def run_steps(now, before, courant, source):
    field = jax.ShapeDtypeStruct((1, NX, CY, CZ), jnp.float32)
    return pl.pallas_call(
        steps_kernel,
        out_shape=(field, field, jax.ShapeDtypeStruct((NX, CY, CZ), jnp.float32)),
        in_specs=[pl.BlockSpec(memory_space=pl.ANY)] * 4,
        out_specs=(pl.BlockSpec(memory_space=pl.ANY),) * 3,
        scratch_shapes=[
            pltpu.VMEM((2, NX + 8, CY + 2 * PAD, CZ), jnp.float32),
            pltpu.VMEM((NX, CY, CZ), jnp.float32),
            pltpu.VMEM((ITERS, NX, CY, CZ), jnp.bfloat16),
            pltpu.VMEM((NX, CY, CZ), jnp.float32),
            pltpu.VMEM((NX, ROWS, CZ), jnp.float32),
            pltpu.VMEM((2, CZ, CZ), jnp.bfloat16),
            pltpu.SemaphoreType.DMA((3 + ITERS,)),
            pltpu.SemaphoreType.DMA((2, ITERS, CHUNKS)),
            pltpu.SemaphoreType.DMA((2, ITERS, CHUNKS)),
            pltpu.SemaphoreType.DMA((3, CHUNKS)),
        ],
        compiler_params=pltpu.CompilerParams(collective_id=0, has_side_effects=True, vmem_limit_bytes=60 * MIB),
        cost_estimate=pl.CostEstimate(flops=400_000_000, bytes_accessed=16_000_000, transcendentals=0),
    )(now, before, courant, source)


PARTS = ((0, 384), (384, 384), (768, 256))
ORDERS = ((0, 1, 2), (1, 2, 0), (2, 0, 1))
STRIDES = (32, 4, 1)
NBLK = 512


def image_kernel(blocks, keys, out, mine, other, other_keys, halves, *rest):
    shot = lax.axis_index("shot")
    sub = lax.axis_index("sub")
    core = lax.rem(shot, 2)
    place = (shot // 2, sub // 4, lax.rem(sub, 4))
    dense, got, (swap, send, recv) = rest[:3], (rest[3:6], rest[6:9], rest[9:12]), rest[12:]

    def at(x, z, y, c):
        return (x * 2 + c, z * 4 + y)

    def beside(axis, by):
        there = list(place)
        there[axis] = lax.rem(there[axis] + by, 4)
        return at(*there, core)

    partner = at(*place, 1 - core)
    barrier = pltpu.get_barrier_semaphore()
    for device in [partner] + [beside(axis, by) for axis in range(3) for by in (1, 3)]:
        pl.semaphore_signal(barrier, inc=1, device_id=device, device_id_type=MESH)
    pl.semaphore_wait(barrier, 7)

    swaps = [
        pltpu.make_async_remote_copy(
            src_ref=blocks, dst_ref=other, send_sem=swap.at[0], recv_sem=swap.at[1], device_id=partner, device_id_type=MESH
        ),
        pltpu.make_async_remote_copy(
            src_ref=keys, dst_ref=other_keys, send_sem=swap.at[2], recv_sem=swap.at[3], device_id=partner, device_id_type=MESH
        ),
    ]
    own = pltpu.make_async_copy(blocks, mine, swap.at[4])
    for copy in swaps:
        copy.start()
    own.start()
    own.wait()

    def split(ref, base):
        def body(i, _):
            rows = pl.ds(pl.multiple_of(i * 32, 32), 32)
            v = ref[rows, :]
            hi = bf(v)
            there = pl.ds(pl.multiple_of(base + i * 32, 32), 32)
            halves[0, there, :] = hi
            halves[1, there, :] = bf(v - f32(hi))
            return 0

        lax.fori_loop(0, NBLK // 32, body, 0)

    split(mine, 0)
    for copy in swaps:
        copy.wait_recv()
    split(other, NBLK)

    row = lax.broadcasted_iota(jnp.int32, (256, 1), 0)

    def group(p, dest):
        a1, a2, a3 = ORDERS[p]
        tile = dest * STRIDES[a1] + (row // 64) * STRIDES[a2] + lax.rem(row // 16, 4) * STRIDES[a3] + core * 16
        key = tile * TSLOTS + lax.rem(row, 16)
        first, lanes = PARTS[p]
        total = jnp.zeros((256, lanes), jnp.float32)
        for side, named in enumerate((keys, other_keys)):
            pick = bf(f32(key == named[0:1, :]))
            for half in range(2):
                total += jnp.dot(
                    pick,
                    halves[half, side * NBLK : (side + 1) * NBLK, first : first + lanes],
                    preferred_element_type=jnp.float32,
                )
        dense[p][dest] = total.reshape(4, 4, 16, lanes)

    def reduced(p, stage):
        return tuple(place[axis] for axis in ORDERS[p][:stage])

    def half_of(stage, front):
        size = 8 if stage == 2 else 2
        return pl.ds(0 if front else size, size)

    def message(p, stage, kind):
        axis = ORDERS[p][stage]
        by = 1 if kind < 3 else 3
        dest = lax.rem(place[axis] + (2 if kind % 3 == 0 else by), 4)
        return pltpu.make_async_remote_copy(
            src_ref=dense[p].at[(*reduced(p, stage), dest, half_of(stage, kind in (0, 2, 4)))],
            dst_ref=got[p][stage].at[kind],
            send_sem=send.at[p, stage, kind],
            recv_sem=recv.at[p, stage, kind],
            device_id=beside(axis, by),
            device_id_type=MESH,
        )

    def add(p, stage, dest, front, kind):
        where = (*reduced(p, stage), dest, half_of(stage, front))
        dense[p][where] = dense[p][where] + got[p][stage][kind]

    def toward(p, stage, by):
        return lax.rem(place[ORDERS[p][stage]] + by, 4)

    for stage in range(3):
        for p in range(3):
            if stage == 0:
                group(p, toward(p, stage, 2))
            message(p, stage, 0).start()
            message(p, stage, 3).start()
        for p in range(3):
            if stage == 0:
                group(p, toward(p, stage, 1))
            message(p, stage, 1).start()
            if stage == 0:
                group(p, toward(p, stage, 3))
            message(p, stage, 4).start()
        for p in range(3):
            message(p, stage, 0).wait_recv()
            add(p, stage, toward(p, stage, 1), True, 0)
            message(p, stage, 2).start()
            message(p, stage, 3).wait_recv()
            add(p, stage, toward(p, stage, 3), False, 3)
            message(p, stage, 5).start()
        for p in range(3):
            if stage == 0:
                group(p, toward(p, stage, 0))
        for p in range(3):
            for kind in (1, 4, 2, 5):
                message(p, stage, kind).wait_recv()
                add(p, stage, toward(p, stage, 0), kind in (2, 4), kind)
    for p in range(3):
        first, lanes = PARTS[p]
        out[0, :, first : first + lanes] = dense[p][reduced(p, 3)]
    for stage in range(3):
        for p in range(3):
            for kind in range(6):
                message(p, stage, kind).wait_send()
    for copy in swaps:
        copy.wait_send()


def run_image(blocks, keys):
    dense = [pltpu.VMEM((4, 4, 4, TSLOTS, lanes), jnp.float32) for _, lanes in PARTS]
    got = []
    for _, lanes in PARTS:
        got += [
            pltpu.VMEM((6, 2, 4, TSLOTS, lanes), jnp.float32),
            pltpu.VMEM((6, 2, TSLOTS, lanes), jnp.float32),
            pltpu.VMEM((6, TSLOTS // 2, lanes), jnp.float32),
        ]
    block = BY * CZ
    return pl.pallas_call(
        image_kernel,
        out_shape=jax.ShapeDtypeStruct((1, TSLOTS, block), jnp.float32),
        in_specs=[pl.BlockSpec(memory_space=pl.ANY), pl.BlockSpec(memory_space=pltpu.VMEM)],
        out_specs=pl.BlockSpec(memory_space=pltpu.VMEM),
        scratch_shapes=[
            pltpu.VMEM((NBLK, block), jnp.float32),
            pltpu.VMEM((NBLK, block), jnp.float32),
            pltpu.VMEM((8, NBLK), jnp.int32),
            pltpu.VMEM((2, 2 * NBLK, block), jnp.bfloat16),
            *dense,
            *got,
            pltpu.SemaphoreType.DMA((5,)),
            pltpu.SemaphoreType.DMA((3, 3, 6)),
            pltpu.SemaphoreType.DMA((3, 3, 6)),
        ],
        compiler_params=pltpu.CompilerParams(collective_id=1, has_side_effects=True, vmem_limit_bytes=60 * MIB),
        cost_estimate=pl.CostEstimate(flops=4_000_000_000, bytes_accessed=4_000_000, transcendentals=0),
    )(blocks, keys)


def on_device(wave_now, wave_before, courant, source_waves, tile_ids, slot_ids):
    last, prior, partial = run_steps(wave_now, wave_before, courant, source_waves)
    keys = tile_ids.reshape(1, NBLK) * TSLOTS + slot_ids.reshape(1, NBLK)
    keys = jnp.broadcast_to(keys, (8, NBLK))
    return last, prior, run_image(partial.reshape(NBLK, BY * CZ), keys)


def solution(mesh):
    return jax.shard_map(
        on_device,
        mesh=mesh,
        in_specs=(
            P("shot", "sub"),
            P("shot", "sub"),
            P("shot", "sub"),
            P(None, "shot", "sub"),
            P("shot", "sub", None),
            P("shot", "sub"),
        ),
        out_specs=(
            P("shot", "sub"),
            P("shot", "sub"),
            P(("shot", "sub")),
        ),
        check_vma=False,
    )
```

time: 788 us -> 103 us (0.13)
  waiting for transfers between devices: 701 us -> 0 us
  Pallas kernels: 0 us -> 94.8 us
  other arithmetic: 33.8 us -> 0.01 us
  starting transfers between devices: 24.3 us -> 0 us
  between operations: 14.3 us -> 0.69 us
  matrix products: 9.3 us -> 0 us
    reduce_scatter x1 -> x0, waiting for transfers between devices: 662 us -> none  [on_device(): lax.psum_scatter(jnp.dot(picker.T, blocks, precision=lax.Precision.HIGHES...]
    pallas_call x0 -> x2, Pallas kernels: none -> 94.8 us  [the longest x1 51.8 us: run_steps(): pl.pallas_call(steps_kernel, out_shape=(field, field, jax.ShapeDtypeStruc...]
    ppermute x8 -> x0, waiting for transfers between devices: 39.2 us -> none  [the longest x4 25.9 us: with_halo(): lax.ppermute(head, axis, [((i + 1) % count, i) for i in range(ends)])]
    add x5 -> x1, other arithmetic: 33.8 us -> 0.01 us  [on_device(): keys = tile_ids.reshape(1, NBLK) * TSLOTS + slot_ids.reshape(1, NBLK)]
    ppermute x8 -> x0, starting transfers between devices: 24.3 us -> none  [the longest x4 19.1 us: with_halo(): lax.ppermute(tail, axis, [(i, (i + 1) % count) for i in range(ends)])]
    dot_general x1 -> x0, matrix products: 9.3 us -> none  [on_device(): jnp.dot(picker.T, blocks, precision=lax.Precision.HIGHEST, preferred_elem...]
  transfers between devices with their start and end apart: 9 -> 0, of which waited for: 9 -> 0; matrix products, arithmetic and copies ran while one was open for 0% -> 0% of each run, Pallas kernels for 0% -> 0%
where the time goes in v1:
time: 103 us
  Pallas kernels  94.8 us (92%)
  local copies, waits for them, and re-layouts  7.76 us (8%)
    pallas_call x1, Pallas kernels, run_steps(): pl.pallas_call(steps_kernel, out_shape=(field, field, jax.ShapeDtypeStruc...  51.8 us
    pallas_call x1, Pallas kernels, run_image(): pl.pallas_call(image_kernel, out_shape=jax.ShapeDtypeStruct((1, TSLOTS, b...  43 us
    unnamed x13, local copies, waits for them, and re-layouts  4.31 us
    reshape x1, local copies, waits for them, and re-layouts, on_device(): return (last, prior, run_image(partial.reshape(NBLK, BY * CZ), keys))  2.84 us

profile of v1, /device:TPU:0, one launch (start us, length us, event | category | flops | bytes accessed | tf_op | source)
XLA Modules:
  0.0 103.2 jit_solution(10771654605012606701)
XLA Ops:
  0.6 51.8 %shard_map.85 = (f32[1,16,128,256]{3,2,1,0:T(8,128)}, f32[1,16,128,256]{3,2,1,0:T(8,128)}, f32[16,128,256]{2,1,0:T(8,128)}) custom-call(f32[1,16,128,256]{3,2,1,0:T(8,128)} %now.1, f32[1,16,128,256]{3,2,1,0:T(8,128)} %before.1, f32[1,16,128,256]{3,2,1,0:T(8,128)} %courant.1, bf16[4,1,16,128,256]{4,3,2,1,0:T(8,128)(2,1)} %source.1), custom_call_target="tpu_custom_call" | custom-call | flops 400000000 | bytes 16000000 | tf_op jit(solution)/shard_map/pallas_call | solution.py:236
  52.4 0.0 copy-start.3
  52.4 0.0 copy-start.4
  52.4 2.8 %reshape.24.blocks = f32[512,1024]{1,0:T(8,128)} reshape(f32[16,128,256]{2,1,0:T(8,128)} %get-tuple-element.8) | data formatting | bytes 4194304 | tf_op jit(solution)/shard_map/reshape | solution.py:434
  55.3 0.0 copy-done.3
  55.3 0.0 copy-done.4
  55.3 0.6 broadcast_in_dim.8.keys
  55.9 0.0 copy-start.1
  55.9 43.0 %shard_map.86 = f32[1,16,1024]{2,1,0:T(8,128)} custom-call(f32[512,1024]{1,0:T(8,128)} %reshape.24.blocks, s32[8,512]{1,0:T(8,128)} %broadcast_in_dim.8.keys), custom_call_target="tpu_custom_call" | custom-call | flops 4000000000 | bytes 4000000 | tf_op jit(solution)/shard_map/pallas_call | solution.py:409
  98.9 0.0 copy-done.1
  98.9 0.0 copy-start
  99.0 1.3 %copy.12 = f32[1,16,128,256]{3,2,1,0:T(8,128)} copy(f32[1,16,128,256]{3,2,1,0:T(8,128)S(1)} %copy-done.1) | data formatting | bytes 4194304
  100.3 1.0 copy-done
  101.3 0.0 copy-start.2
  101.3 1.3 %copy.13 = f32[1,16,128,256]{3,2,1,0:T(8,128)} copy(f32[1,16,128,256]{3,2,1,0:T(8,128)S(1)} %copy-done) | data formatting | bytes 4194304
  102.6 0.0 copy-done.2
  102.6 0.6 copy.14
  (1 shorter events, 0.0 us)
Async XLA Ops:
  52.4 2.9 %copy-start.3 = (s32[1,512]{1,0:T(1,128)S(1)}, s32[1,512]{1,0:T(1,128)}, u32[]{:S(2)}) copy-start(s32[1,512]{1,0:T(1,128)} %param.11) | copy-start | bytes 6148
  52.4 2.9 %copy-start.4 = (s32[1,512,1]{1,2,0:T(1,128)S(1)}, s32[1,512,1]{1,2,0:T(1,128)}, u32[]{:S(2)}) copy-start(s32[1,512,1]{1,2,0:T(1,128)} %param.10) | copy-start | bytes 6148
  55.9 43.0 %copy-start.1 = (f32[1,16,128,256]{3,2,1,0:T(8,128)S(1)}, f32[1,16,128,256]{3,2,1,0:T(8,128)}, u32[]{:S(2)}) copy-start(f32[1,16,128,256]{3,2,1,0:T(8,128)} %get-tuple-element.12) | copy-start | bytes 6291460
  98.9 2.3 %copy-start = (f32[1,16,128,256]{3,2,1,0:T(8,128)S(1)}, f32[1,16,128,256]{3,2,1,0:T(8,128)}, u32[]{:S(2)}) copy-start(f32[1,16,128,256]{3,2,1,0:T(8,128)} %get-tuple-element.13) | copy-start | bytes 6291460
  101.3 1.3 %copy-start.2 = (f32[1,16,1024]{2,1,0:T(8,128)S(1)}, f32[1,16,1024]{2,1,0:T(8,128)}, u32[]{:S(2)}) copy-start(f32[1,16,1024]{2,1,0:T(8,128)} %shard_map.86) | copy-start | bytes 196612

commit v2 on v0

v2 whole, which is shorter than its diff:
```python
import jax
import jax.numpy as jnp
from jax import lax
from jax.experimental import pallas as pl
from jax.experimental.pallas import tpu as pltpu
from jax.sharding import PartitionSpec as P

ITERS = 4
BY = 4
TSLOTS = 16
MESH = pl.DeviceIdType.MESH
W = (-205.0 / 72.0, 8.0 / 5.0, -1.0 / 5.0, 8.0 / 315.0, -1.0 / 560.0)

NX, CY, CZ = 16, 128, 256
ROWS = 16
CHUNKS = CY // ROWS
PAD = 8
MIB = 1024 * 1024
STEP_BLOCKS = NX * ROWS // BY
LANES = 128
NBLK = NX * CY // BY
XB = 2
GROUP = 8
WIDE = ROWS + 2 * PAD
INNER, OUTER = (4, 8), (0, 12)
PARTS = ((0, 3), (3, 3), (6, 2))
ORDERS = ((0, 1, 2), (1, 2, 0), (2, 0, 1))


def bf(v):
    return v.astype(jnp.bfloat16)


def f32(v):
    return v.astype(jnp.float32)


def kernel(now, before, courant, source, tiles_here, slots_here, last, prior, out, wave, speed, src, part, other, zpart, band, across, keys, other_keys, rhs, dense, *rest):
    ring, direct, final, (load, send, recv, store, swap, post, mail) = rest[0:3], rest[3:6], rest[6:9], rest[9:]
    shot = lax.axis_index("shot")
    sub = lax.axis_index("sub")
    count = lax.axis_size("sub")
    core = lax.rem(shot, 2)
    place = (shot // 2, sub // 4, lax.rem(sub, 4))
    has_left = sub > 0
    has_right = sub < count - 1
    left = (shot, jnp.maximum(sub - 1, 0))
    right = (shot, jnp.minimum(sub + 1, count - 1))

    def beside(axis, by):
        x, z, y = (lax.rem(c + by, 4) if a == axis else c for a, c in enumerate(place))
        return (x * 2 + core, z * 4 + y)

    partner = (shot + 1 - 2 * core, sub)

    inner = (pl.ds(4, NX), pl.ds(PAD, CY))
    loads = [
        pltpu.make_async_copy(now.at[0], wave.at[(0, *inner)], load.at[0]),
        pltpu.make_async_copy(before.at[0], wave.at[(1, *inner)], load.at[1]),
        pltpu.make_async_copy(courant.at[0], speed, load.at[2]),
    ]
    loads += [pltpu.make_async_copy(source.at[t, 0], src.at[t], load.at[3 + t]) for t in range(ITERS)]
    for copy in loads:
        copy.start()

    barrier = pltpu.get_barrier_semaphore()

    @pl.when(has_left)
    def _():
        pl.semaphore_signal(barrier, inc=1, device_id=left, device_id_type=MESH)

    @pl.when(has_right)
    def _():
        pl.semaphore_signal(barrier, inc=1, device_id=right, device_id_type=MESH)

    for device in [partner] + [beside(axis, by) for axis in range(3) for by in (1, 2, 3)]:
        pl.semaphore_signal(barrier, inc=1, device_id=device, device_id_type=MESH)

    edge = jnp.zeros((2, 4, CY, CZ), jnp.float32)

    @pl.when(jnp.logical_not(has_left))
    def _():
        wave[:, 0:4, PAD : PAD + CY, :] = edge

    @pl.when(jnp.logical_not(has_right))
    def _():
        wave[:, NX + 4 : NX + 8, PAD : PAD + CY, :] = edge

    strip = jnp.zeros((2, NX, PAD, CZ), jnp.float32)
    wave[:, 4 : NX + 4, 0:PAD, :] = strip
    wave[:, 4 : NX + 4, PAD + CY :, :] = strip
    def taps(gap):
        weights = jnp.zeros(gap.shape, jnp.float32)
        for k in range(1, 5):
            weights = jnp.where(gap == k, W[k] / W[1], weights)
        return weights

    def grid(shape, axis):
        return lax.broadcasted_iota(jnp.int32, shape, axis)

    band[...] = bf(taps(jnp.abs(grid((CZ, CZ), 0) - grid((CZ, CZ), 1))))
    shape = (GROUP * ROWS, GROUP * WIDE)
    gap = jnp.abs(lax.rem(grid(shape, 0), ROWS) + PAD - lax.rem(grid(shape, 1), WIDE))
    across[...] = bf(jnp.where(grid(shape, 0) // ROWS == grid(shape, 1) // WIDE, taps(gap), 0.0))

    at_block = lax.broadcasted_iota(jnp.int32, (1, NBLK), 1)
    at_chunk = lax.broadcasted_iota(jnp.int32, (CHUNKS, NBLK), 0)
    spread = bf(
        f32(
            lax.rem(lax.broadcasted_iota(jnp.int32, (NBLK, LANES), 1), STEP_BLOCKS)
            == lax.broadcasted_iota(jnp.int32, (NBLK, LANES), 0) // (CY // BY) * (ROWS // BY)
            + lax.rem(lax.broadcasted_iota(jnp.int32, (NBLK, LANES), 0), ROWS // BY)
        )
    )
    in_chunk = lax.rem(at_block // (ROWS // BY), CHUNKS) == at_chunk
    named_tile, named_slot = (
        jnp.dot(bf(jnp.where(in_chunk, f32(ref[...]), 0.0)), spread, preferred_element_type=jnp.float32)
        for ref in (tiles_here, slots_here)
    )
    keys[...] = named_tile * TSLOTS + named_slot

    pl.semaphore_wait(barrier, jnp.where(has_left, 1, 0) + jnp.where(has_right, 1, 0) + 10)

    def to_left(t, j, source_ref=None):
        b = lax.rem(t, 2)
        rows = pl.ds(PAD + j * ROWS, ROWS)
        return pltpu.make_async_remote_copy(
            src_ref=source_ref if source_ref is not None else wave.at[b, pl.ds(4, 4), rows],
            dst_ref=wave.at[b, pl.ds(NX + 4, 4), rows],
            send_sem=send.at[0, t, j],
            recv_sem=recv.at[0, t, j],
            device_id=left,
            device_id_type=MESH,
        )

    def to_right(t, j, source_ref=None):
        b = lax.rem(t, 2)
        rows = pl.ds(PAD + j * ROWS, ROWS)
        return pltpu.make_async_remote_copy(
            src_ref=source_ref if source_ref is not None else wave.at[b, pl.ds(NX, 4), rows],
            dst_ref=wave.at[b, pl.ds(0, 4), rows],
            send_sem=send.at[1, t, j],
            recv_sem=recv.at[1, t, j],
            device_id=right,
            device_id_type=MESH,
        )

    def first(j, _):
        rows = pl.ds(j * ROWS, ROWS)

        @pl.when(has_left)
        def _():
            to_left(0, j, now.at[0, pl.ds(0, 4), rows]).start()

        @pl.when(has_right)
        def _():
            to_right(0, j, now.at[0, pl.ds(NX - 4, 4), rows]).start()

        return 0

    lax.fori_loop(0, CHUNKS, first, 0)

    key_swap = pltpu.make_async_remote_copy(
        src_ref=keys, dst_ref=other_keys, send_sem=swap.at[0, CHUNKS], recv_sem=swap.at[1, CHUNKS], device_id=partner, device_id_type=MESH
    )
    key_swap.start()
    dense[...] = jnp.zeros_like(dense)
    part[...] = jnp.zeros_like(part)

    for copy in loads[:3]:
        copy.wait()

    def group(t, j, places):
        cur = lax.rem(t, 2)
        nxt = 1 - cur
        window = pl.ds(pl.multiple_of(j * ROWS, ROWS), WIDE)
        rows = pl.ds(pl.multiple_of(PAD + j * ROWS, 8), ROWS)
        plain = pl.ds(pl.multiple_of(j * ROWS, ROWS), ROWS)

        v = jnp.concatenate([wave[cur, 4 + a : 8 + a, window, :] for a in places], axis=0).reshape(GROUP * WIDE, CZ)
        hi = bf(v)
        lo = bf(v - f32(hi))
        deep = jnp.dot(hi, band[...], preferred_element_type=jnp.float32)
        deep += jnp.dot(lo, band[...], preferred_element_type=jnp.float32)
        flat = jnp.dot(across[...], hi, preferred_element_type=jnp.float32)
        flat += jnp.dot(across[...], lo, preferred_element_type=jnp.float32)
        zpart[...] = deep.reshape(GROUP, WIDE, CZ)[:, PAD : PAD + ROWS] + flat.reshape(GROUP, ROWS, CZ)

        for i in range(0, GROUP, XB):
            x = places[i // 4] + i % 4
            here = slice(x, x + XB)
            center = wave[cur, x + 4 : x + 4 + XB, rows, :]
            lap = 3.0 * W[0] / W[1] * center + zpart[i : i + XB]
            for k in range(1, 5):
                pair = wave[cur, x + 4 + k : x + 4 + k + XB, rows, :] + wave[cur, x + 4 - k : x + 4 - k + XB, rows, :]
                lap += pair if k == 1 else W[k] / W[1] * pair
            after = 2.0 * center - wave[nxt, x + 4 : x + 4 + XB, rows, :] + W[1] * speed[here, plain, :] * lap
            wave[nxt, x + 4 : x + 4 + XB, rows, :] = after
            term = (f32(src[t, here, plain, :]) * after).reshape(XB * ROWS, CZ)
            there = slice(x * ROWS, (x + XB) * ROWS)
            for h in range(CZ // LANES):
                piece = term[:, h * LANES : (h + 1) * LANES]
                part[j, h, there, :] = part[j, h, there, :] + piece

    def edges(t, j):
        @pl.when(has_left)
        def _():
            to_right(t, j).wait_recv()

            @pl.when(t > 0)
            def _():
                to_left(t, j).wait_send()

        @pl.when(has_right)
        def _():
            to_left(t, j).wait_recv()

            @pl.when(t > 0)
            def _():
                to_right(t, j).wait_send()

        group(t, j, OUTER)

        @pl.when(t < ITERS - 1)
        def _():
            @pl.when(has_left)
            def _():
                to_left(t + 1, j).start()

            @pl.when(has_right)
            def _():
                to_right(t + 1, j).start()

    def last_copy(j):
        rows = pl.ds(pl.multiple_of(PAD + j * ROWS, 8), ROWS)
        plain = pl.ds(pl.multiple_of(j * ROWS, ROWS), ROWS)
        return pltpu.make_async_copy(wave.at[ITERS % 2, pl.ds(4, NX), rows], last.at[0, :, plain], store.at[j])

    prior_copy = pltpu.make_async_copy(wave.at[((ITERS + 1) % 2, *inner)], prior.at[0], store.at[CHUNKS])

    def give(j):
        return pltpu.make_async_remote_copy(
            src_ref=part.at[j], dst_ref=other.at[j], send_sem=swap.at[0, j], recv_sem=swap.at[1, j], device_id=partner, device_id_type=MESH
        )

    slot_row = f32(lax.broadcasted_iota(jnp.int32, (256, 1), 0))
    lane = lax.broadcasted_iota(jnp.int32, (1, LANES), 1)

    def fold(j):
        give(j).wait_recv()
        for r in range(BY):
            for h in range(CZ // LANES):
                both = jnp.concatenate(
                    [ref[j, h, pl.ds(r, STEP_BLOCKS, stride=BY), :] for ref in (part, other)], axis=0
                )
                hi = bf(both)
                rhs[r, 0:LANES, h * LANES : (h + 1) * LANES] = hi
                rhs[r, LANES : 2 * LANES, h * LANES : (h + 1) * LANES] = bf(both - f32(hi))
        named = jnp.where(lane < STEP_BLOCKS, keys[pl.ds(j, 1), :], other_keys[pl.ds(j, 1), :])
        named = jnp.concatenate([named, named], axis=1)

        def tiles(x, _):
            pick = bf(f32(named - f32(x * 512 + core * 256) == slot_row))
            for r in range(BY):
                sums = jnp.dot(pick, rhs[r], preferred_element_type=jnp.float32)
                for h in range(CZ // LANES):
                    tile = CZ // LANES * r + h
                    dense[tile, x] += sums[:, h * LANES : (h + 1) * LANES].reshape(4, 4, TSLOTS, LANES)
            return 0

        lax.fori_loop(0, 4, tiles, 0)

    def one_step(t, _):
        for s in range(ITERS - 1):

            @pl.when(t == s)
            def _():
                loads[3 + s].wait()

        def one_chunk(j, _):
            group(t, j, INNER)
            edges(t, j)

            @pl.when(jnp.logical_and(t == ITERS - 2, j > 0))
            def _():
                group(ITERS - 1, j - 1, INNER)

            return 0

        lax.fori_loop(0, CHUNKS, one_chunk, 0)
        return 0

    loads[2 + ITERS].wait()
    lax.fori_loop(0, ITERS - 1, one_step, 0)
    prior_copy.start()
    group(ITERS - 1, CHUNKS - 1, INNER)
    key_swap.wait_recv()

    def last_chunk(j, _):
        edges(ITERS - 1, j)
        give(j).start()
        last_copy(j).start()

        @pl.when(j > 0)
        def _():
            fold(j - 1)

        return 0

    lax.fori_loop(0, CHUNKS, last_chunk, 0)
    fold(CHUNKS - 1)

    def toward(p, stage, by):
        return lax.rem(place[ORDERS[p][stage]] + by, 4)

    def block(p, stage, dest, half=None):
        index = [slice(None)] * 3
        for axis in ORDERS[p][:stage]:
            index[axis] = place[axis]
        index[ORDERS[p][stage]] = dest
        if half is not None:
            index[ORDERS[p][stage + 1]] = pl.ds(2 * half, 2)
        return (pl.ds(*PARTS[p]), *index)

    def message(p, kind):
        by = 1 if kind < 3 else 3
        return pltpu.make_async_remote_copy(
            src_ref=dense.at[block(p, 0, toward(p, 0, 2 if kind % 3 == 0 else by), 0 if kind in (0, 2, 4) else 1)],
            dst_ref=ring[p].at[kind],
            send_sem=post.at[p, kind],
            recv_sem=mail.at[p, kind],
            device_id=beside(ORDERS[p][0], by),
            device_id_type=MESH,
        )

    def straight(p, stage, by):
        return pltpu.make_async_remote_copy(
            src_ref=dense.at[block(p, stage, toward(p, stage, by))],
            dst_ref=(direct, final)[stage - 1][p].at[by - 1],
            send_sem=post.at[p, 3 + 3 * stage + by - 1],
            recv_sem=mail.at[p, 3 + 3 * stage + by - 1],
            device_id=beside(ORDERS[p][stage], by),
            device_id_type=MESH,
        )

    def add(where, *terms):
        total = dense[where]
        for term in terms:
            total = total + term
        dense[where] = total

    for p in range(3):
        message(p, 0).start()
        message(p, 3).start()
    for p in range(3):
        message(p, 1).start()
        message(p, 4).start()
    for p in range(3):
        message(p, 0).wait_recv()
        add(block(p, 0, toward(p, 0, 1), 0), ring[p][0])
        message(p, 2).start()
        message(p, 3).wait_recv()
        add(block(p, 0, toward(p, 0, 3), 1), ring[p][3])
        message(p, 5).start()
    for p in range(3):
        for kind in (1, 4, 2, 5):
            message(p, kind).wait_recv()
        add(block(p, 0, toward(p, 0, 0), 0), ring[p][2], ring[p][4])
        add(block(p, 0, toward(p, 0, 0), 1), ring[p][1], ring[p][5])
        for by in (2, 1, 3):
            straight(p, 1, by).start()
    for stage in (1, 2):
        for p in range(3):
            for by in (2, 1, 3):
                straight(p, stage, by).wait_recv()
            got = (direct, final)[stage - 1][p]
            add(block(p, stage, toward(p, stage, 0)), got[0], got[1], got[2])
            if stage == 1:
                for by in (2, 1, 3):
                    straight(p, 2, by).start()
    for tile in range(BY * CZ // LANES):
        out[0, :, tile * LANES : (tile + 1) * LANES] = dense[(tile, *place)]

    for p in range(3):
        for kind in range(6):
            message(p, kind).wait_send()
        for stage in (1, 2):
            for by in (1, 2, 3):
                straight(p, stage, by).wait_send()

    def finish(j, _):
        last_copy(j).wait()
        give(j).wait_send()
        rows = pl.ds(j * ROWS, ROWS)

        @pl.when(has_left)
        def _():
            to_left(0, j, now.at[0, pl.ds(0, 4), rows]).wait_send()

        @pl.when(has_right)
        def _():
            to_right(0, j, now.at[0, pl.ds(NX - 4, 4), rows]).wait_send()

        return 0

    lax.fori_loop(0, CHUNKS, finish, 0)
    key_swap.wait_send()
    prior_copy.wait()


def run(now, before, courant, source, tiles_here, slots_here):
    field = pltpu.VMEM((1, NX, CY, CZ), jnp.float32)
    ring, direct, final = [], [], []
    for order, (_, tiles) in zip(ORDERS, PARTS):
        sizes = [2 if axis == order[1] else 4 for axis in range(3) if axis != order[0]]
        ring.append(pltpu.VMEM((6, tiles, *sizes, TSLOTS, LANES), jnp.float32))
        direct.append(pltpu.VMEM((3, tiles, 4, TSLOTS, LANES), jnp.float32))
        final.append(pltpu.VMEM((3, tiles, TSLOTS, LANES), jnp.float32))
    halves = CZ // LANES
    return pl.pallas_call(
        kernel,
        out_shape=(field, field, pltpu.VMEM((1, TSLOTS, BY * CZ), jnp.float32)),
        in_specs=[pl.BlockSpec(memory_space=pl.ANY)] * 4 + [pl.BlockSpec(memory_space=pltpu.VMEM)] * 2,
        out_specs=(pl.BlockSpec(memory_space=pltpu.VMEM),) * 3,
        scratch_shapes=[
            pltpu.VMEM((2, NX + 8, CY + 2 * PAD, CZ), jnp.float32),
            pltpu.VMEM((NX, CY, CZ), jnp.float32),
            pltpu.VMEM((ITERS, NX, CY, CZ), jnp.bfloat16),
            pltpu.VMEM((CHUNKS, halves, NX * ROWS, LANES), jnp.float32),
            pltpu.VMEM((CHUNKS, halves, NX * ROWS, LANES), jnp.float32),
            pltpu.VMEM((GROUP, ROWS, CZ), jnp.float32),
            pltpu.VMEM((CZ, CZ), jnp.bfloat16),
            pltpu.VMEM((GROUP * ROWS, GROUP * WIDE), jnp.bfloat16),
            pltpu.VMEM((CHUNKS, LANES), jnp.float32),
            pltpu.VMEM((CHUNKS, LANES), jnp.float32),
            pltpu.VMEM((BY, 4 * STEP_BLOCKS, CZ), jnp.bfloat16),
            pltpu.VMEM((BY * halves, 4, 4, 4, TSLOTS, LANES), jnp.float32),
            *ring,
            *direct,
            *final,
            pltpu.SemaphoreType.DMA((3 + ITERS,)),
            pltpu.SemaphoreType.DMA((2, ITERS, CHUNKS)),
            pltpu.SemaphoreType.DMA((2, ITERS, CHUNKS)),
            pltpu.SemaphoreType.DMA((CHUNKS + 1,)),
            pltpu.SemaphoreType.DMA((2, CHUNKS + 1)),
            pltpu.SemaphoreType.DMA((3, 12)),
            pltpu.SemaphoreType.DMA((3, 12)),
        ],
        compiler_params=pltpu.CompilerParams(collective_id=0, has_side_effects=True, vmem_limit_bytes=59 * MIB),
        cost_estimate=pl.CostEstimate(flops=5_000_000_000, bytes_accessed=16_000_000, transcendentals=0),
    )(now, before, courant, source, tiles_here, slots_here)


def keep(*refs):
    semaphores = refs[6]
    copies = [pltpu.make_async_copy(refs[i], refs[3 + i], semaphores.at[i]) for i in range(3)]
    for copy in copies:
        copy.start()
    for copy in copies:
        copy.wait()


def on_device(wave_now, wave_before, courant, source_waves, tile_ids, slot_ids):
    results = run(wave_now, wave_before, courant, source_waves, tile_ids.reshape(1, NBLK), slot_ids.reshape(1, NBLK))
    return pl.pallas_call(
        keep,
        out_shape=tuple(jax.ShapeDtypeStruct(v.shape, v.dtype) for v in results),
        in_specs=[pl.BlockSpec(memory_space=pl.ANY)] * 3,
        out_specs=(pl.BlockSpec(memory_space=pl.ANY),) * 3,
        scratch_shapes=[pltpu.SemaphoreType.DMA((3,))],
        compiler_params=pltpu.CompilerParams(vmem_limit_bytes=MIB),
    )(*results)


def solution(mesh):
    return jax.shard_map(
        on_device,
        mesh=mesh,
        in_specs=(
            P("shot", "sub"),
            P("shot", "sub"),
            P("shot", "sub"),
            P(None, "shot", "sub"),
            P("shot", "sub", None),
            P("shot", "sub"),
        ),
        out_specs=(
            P("shot", "sub"),
            P("shot", "sub"),
            P(("shot", "sub")),
        ),
        check_vma=False,
    )
```

time: 788 us -> 90.8 us (0.12)
  waiting for transfers between devices: 701 us -> 0 us
  Pallas kernels: 0 us -> 89.6 us
  other arithmetic: 33.8 us -> 0 us
  starting transfers between devices: 24.3 us -> 0 us
  between operations: 14.3 us -> 0.64 us
  matrix products: 9.3 us -> 0 us
    reduce_scatter x1 -> x0, waiting for transfers between devices: 662 us -> none  [on_device(): lax.psum_scatter(jnp.dot(picker.T, blocks, precision=lax.Precision.HIGHES...]
    pallas_call x0 -> x2, Pallas kernels: none -> 89.6 us  [the longest x1 87.6 us: run(): pl.pallas_call(kernel, out_shape=(field, field, pltpu.VMEM((1, TSLOTS, BY...]
    ppermute x8 -> x0, waiting for transfers between devices: 39.2 us -> none  [the longest x4 25.9 us: with_halo(): lax.ppermute(head, axis, [((i + 1) % count, i) for i in range(ends)])]
    add x5 -> x0, other arithmetic: 33.8 us -> none  [the longest x3 22 us: on_device(): after = 2.0 * current - before + courant * laplace(padded)]
    ppermute x8 -> x0, starting transfers between devices: 24.3 us -> none  [the longest x4 19.1 us: with_halo(): lax.ppermute(tail, axis, [(i, (i + 1) % count) for i in range(ends)])]
    dot_general x1 -> x0, matrix products: 9.3 us -> none  [on_device(): jnp.dot(picker.T, blocks, precision=lax.Precision.HIGHEST, preferred_elem...]
  transfers between devices with their start and end apart: 9 -> 0, of which waited for: 9 -> 0; matrix products, arithmetic and copies ran while one was open for 0% -> 0% of each run, Pallas kernels for 0% -> 0%
where the time goes in v2:
time: 90.8 us; the launch traced here: 90.3 us
  Pallas kernels  89.6 us (99%)
    pallas_call x1, Pallas kernels, run(): pl.pallas_call(kernel, out_shape=(field, field, pltpu.VMEM((1, TSLOTS, BY...  87.6 us
    pallas_call x1, Pallas kernels, on_device(): pl.pallas_call(keep, out_shape=tuple((jax.ShapeDtypeStruct(v.shape, v.dty...  2.04 us

profile of v2, /device:TPU:0, one launch (start us, length us, event | category | flops | bytes accessed | tf_op | source)
XLA Modules:
  0.0 90.3 jit_solution(11411501052988119895)
XLA Ops:
  0.6 87.6 %shard_map.85 = (f32[1,16,128,256]{3,2,1,0:T(8,128)S(1)}, f32[1,16,128,256]{3,2,1,0:T(8,128)S(1)}, f32[1,16,1024]{2,1,0:T(8,128)S(1)}) custom-call(f32[1,16,128,256]{3,2,1,0:T(8,128)} %now.1, f32[1,16,128,256]{3,2,1,0:T(8,128)} %before.1, f32[1,16,128,256]{3,2,1,0:T(8,128)} %courant.1, bf16[4,1,16,128,256]{4,3,2,1,0:T(8,128)(2,1)} %source.1, ...), custom_call_target="tpu_custom_call" | custom-call | flops 5000000000 | bytes 16000000 | tf_op jit(solution)/shard_map/pallas_call | solution.py:420
  88.2 2.0 %shard_map.86 = (f32[1,16,128,256]{3,2,1,0:T(8,128)}, f32[1,16,128,256]{3,2,1,0:T(8,128)}, f32[1,16,1024]{2,1,0:T(8,128)}) custom-call(f32[1,16,128,256]{3,2,1,0:T(8,128)S(1)} %get-tuple-element.6.refs_0_, f32[1,16,128,256]{3,2,1,0:T(8,128)S(1)} %get-tuple-element.7.refs_1_, f32[1,16,1024]{2,1,0:T(8,128)S(1)} %get-tuple-element.8.refs_2_), custom_call_target="tpu_custom_call" | custom-call | tf_op jit(solution)/shard_map/pallas_call | solution.py:465

commit v3 on v2

v3 whole, which is shorter than its diff:
```python
import functools

import jax
import jax.numpy as jnp
from jax import lax
from jax.experimental import pallas as pl
from jax.experimental.pallas import tpu as pltpu
from jax.sharding import PartitionSpec as P

MESH = pl.DeviceIdType.MESH
MIB = 1024 * 1024
ITERS = 4
BY = 4
TSLOTS = 16
W = (-205.0 / 72.0, 8.0 / 5.0, -1.0 / 5.0, 8.0 / 315.0, -1.0 / 560.0)

NX, CY, CZ = 16, 128, 256
NBLK = NX * CY // BY
LANES = 128
HALVES = CZ // LANES
ROWS = 16
CHUNKS = CY // ROWS
PAD = 8
WIDE = ROWS + 2 * PAD
GROUP = 8
INNER, OUTER = 0, 1
LAYERS = ((4, 8), (0, 12))
XB = 2
HELD = GROUP * ROWS // BY
PAIR = 2 * HELD
FOLDS = CHUNKS // 2
PARTS = (
    (0, 2, (0, 1, 2)),
    (2, 2, (1, 0, 2)),
    (4, 1, (2, 0, 1)),
    (5, 1, (2, 1, 0)),
    (6, 1, (0, 1, 2)),
    (7, 1, (1, 0, 2)),
)
EARLY, LATE = (0, 1), (2, 3, 4, 5)


def bf(v):
    return v.astype(jnp.bfloat16)


def f32(v):
    return v.astype(jnp.float32)


def grid(shape, axis):
    return lax.broadcasted_iota(jnp.int32, shape, axis)


def kernel(now, before, courant, source, tiles_here, slots_here, last, prior, out, wave, speed, src, part, other, *rest):
    (zpart, zlast, band, across, keys, other_keys, rhs, dense), rest = rest[:8], rest[8:]
    count_parts = len(PARTS)
    ring, direct, final = (rest[i * count_parts : (i + 1) * count_parts] for i in range(3))
    load, send, recv, store, swap, key_sem, post, mail = rest[3 * count_parts :]
    shot = lax.axis_index("shot")
    sub = lax.axis_index("sub")
    count = lax.axis_size("sub")
    core = lax.rem(shot, 2)
    place = (shot // 2, sub // 4, lax.rem(sub, 4))
    has_left = sub > 0
    has_right = sub < count - 1
    left = (shot, jnp.maximum(sub - 1, 0))
    right = (shot, jnp.minimum(sub + 1, count - 1))
    partner = (shot + 1 - 2 * core, sub)

    def beside(axis, by):
        x, z, y = (lax.rem(c + by, 4) if a == axis else c for a, c in enumerate(place))
        return (x * 2 + core, z * 4 + y)

    barrier = pltpu.get_barrier_semaphore()

    @pl.when(has_left)
    def _():
        pl.semaphore_signal(barrier, inc=1, device_id=left, device_id_type=MESH)

    @pl.when(has_right)
    def _():
        pl.semaphore_signal(barrier, inc=1, device_id=right, device_id_type=MESH)

    for device in [partner] + [beside(axis, by) for axis in range(3) for by in (2, 1, 3)]:
        pl.semaphore_signal(barrier, inc=1, device_id=device, device_id_type=MESH)

    inner = (pl.ds(4, NX), pl.ds(PAD, CY))
    loads = [
        pltpu.make_async_copy(now.at[0], wave.at[(0, *inner)], load.at[0]),
        pltpu.make_async_copy(before.at[0], wave.at[(1, *inner)], load.at[1]),
        pltpu.make_async_copy(courant.at[0], speed, load.at[2]),
    ]
    loads += [pltpu.make_async_copy(source.at[t, 0], src.at[t], load.at[3 + t]) for t in range(ITERS)]
    for copy in loads:
        copy.start()

    edge = jnp.zeros((2, 4, CY, CZ), jnp.float32)

    @pl.when(jnp.logical_not(has_left))
    def _():
        wave[:, 0:4, PAD : PAD + CY, :] = edge

    @pl.when(jnp.logical_not(has_right))
    def _():
        wave[:, NX + 4 : NX + 8, PAD : PAD + CY, :] = edge

    strip = jnp.zeros((2, NX, PAD, CZ), jnp.float32)
    wave[:, 4 : NX + 4, 0:PAD, :] = strip
    wave[:, 4 : NX + 4, PAD + CY :, :] = strip

    def taps(gap):
        weights = jnp.zeros(gap.shape, jnp.float32)
        for k in range(1, 5):
            weights = jnp.where(gap == k, W[k] / W[1], weights)
        return weights

    band[...] = bf(taps(jnp.abs(grid((CZ, CZ), 0) - grid((CZ, CZ), 1))))
    shape = (GROUP * ROWS, GROUP * WIDE)
    gap = jnp.abs(lax.rem(grid(shape, 0), ROWS) + PAD - lax.rem(grid(shape, 1), WIDE))
    across[...] = bf(jnp.where(grid(shape, 0) // ROWS == grid(shape, 1) // WIDE, taps(gap), 0.0))

    pl.semaphore_wait(barrier, jnp.where(has_left, 1, 0) + jnp.where(has_right, 1, 0) + 10)

    def to_left(t, j, source_ref=None):
        b = lax.rem(t, 2)
        rows = pl.ds(PAD + j * ROWS, ROWS)
        return pltpu.make_async_remote_copy(
            src_ref=source_ref if source_ref is not None else wave.at[b, pl.ds(4, 4), rows],
            dst_ref=wave.at[b, pl.ds(NX + 4, 4), rows],
            send_sem=send.at[0, t, j],
            recv_sem=recv.at[0, t, j],
            device_id=left,
            device_id_type=MESH,
        )

    def to_right(t, j, source_ref=None):
        b = lax.rem(t, 2)
        rows = pl.ds(PAD + j * ROWS, ROWS)
        return pltpu.make_async_remote_copy(
            src_ref=source_ref if source_ref is not None else wave.at[b, pl.ds(NX, 4), rows],
            dst_ref=wave.at[b, pl.ds(0, 4), rows],
            send_sem=send.at[1, t, j],
            recv_sem=recv.at[1, t, j],
            device_id=right,
            device_id_type=MESH,
        )

    def first(j, _):
        rows = pl.ds(j * ROWS, ROWS)

        @pl.when(has_left)
        def _():
            to_left(0, j, now.at[0, pl.ds(0, 4), rows]).start()

        @pl.when(has_right)
        def _():
            to_right(0, j, now.at[0, pl.ds(NX - 4, 4), rows]).start()

        return 0

    lax.fori_loop(0, CHUNKS, first, 0)

    def keyed(b):
        x, j, g = b // (CY // BY), lax.rem(b // (ROWS // BY), CHUNKS), lax.rem(b, ROWS // BY)
        outer = jnp.logical_or(x < 4, x >= 12)
        place_in = jnp.where(outer, jnp.where(x < 4, x, x - 8), x - 4)
        return jnp.where(outer, FOLDS, 0) + j // 2, lax.rem(j, 2) * HELD + place_in * (ROWS // BY) + g

    spread = bf(f32(lax.rem(grid((NBLK, LANES), 1), PAIR) == keyed(grid((NBLK, LANES), 0))[1]))
    in_fold = keyed(grid((2 * FOLDS, NBLK), 1))[0] == grid((2 * FOLDS, NBLK), 0)
    named_tile, named_slot = (
        jnp.dot(bf(jnp.where(in_fold, f32(ref[...]), 0.0)), spread, preferred_element_type=jnp.float32)
        for ref in (tiles_here, slots_here)
    )
    keys[...] = named_tile * TSLOTS + named_slot
    key_swap = pltpu.make_async_remote_copy(
        src_ref=keys, dst_ref=other_keys, send_sem=key_sem.at[0], recv_sem=key_sem.at[1], device_id=partner, device_id_type=MESH
    )
    key_swap.start()
    dense[...] = jnp.zeros_like(dense)
    part[...] = jnp.zeros_like(part)

    for copy in loads[:4]:
        copy.wait()

    def mix(t, j, kind):
        cur = lax.rem(t, 2)
        window = pl.ds(pl.multiple_of(j * ROWS, ROWS), WIDE)
        v = jnp.concatenate([wave[cur, 4 + a : 8 + a, window, :] for a in LAYERS[kind]], axis=0).reshape(GROUP * WIDE, CZ)
        hi = bf(v)
        lo = bf(v - f32(hi))
        deep = jnp.dot(hi, band[...], preferred_element_type=jnp.float32)
        deep += jnp.dot(lo, band[...], preferred_element_type=jnp.float32)
        flat = jnp.dot(across[...], hi, preferred_element_type=jnp.float32)
        flat += jnp.dot(across[...], lo, preferred_element_type=jnp.float32)
        return deep.reshape(GROUP, WIDE, CZ)[:, PAD : PAD + ROWS] + flat.reshape(GROUP, ROWS, CZ)

    def update(t, j, kind, mixed, halves):
        cur = lax.rem(t, 2)
        nxt = 1 - cur
        rows = pl.ds(pl.multiple_of(PAD + j * ROWS, 8), ROWS)
        plain = pl.ds(pl.multiple_of(j * ROWS, ROWS), ROWS)
        deep = slice(halves[0] * LANES, (halves[-1] + 1) * LANES)
        block = 2 * XB // len(halves)
        for i in range(0, GROUP, block):
            x = LAYERS[kind][i // 4] + i % 4
            here = slice(x, x + block)
            center = wave[cur, x + 4 : x + 4 + block, rows, deep]
            lap = 3.0 * W[0] / W[1] * center + mixed[i : i + block, :, deep]
            for k in range(1, 5):
                pair = wave[cur, x + 4 + k : x + 4 + k + block, rows, deep] + wave[cur, x + 4 - k : x + 4 - k + block, rows, deep]
                lap += pair if k == 1 else W[k] / W[1] * pair
            after = 2.0 * center - wave[nxt, x + 4 : x + 4 + block, rows, deep] + W[1] * speed[here, plain, deep] * lap
            wave[nxt, x + 4 : x + 4 + block, rows, deep] = after
            term = (f32(src[t, here, plain, deep]) * after).reshape(block * ROWS, len(halves) * LANES)
            there = slice(i * ROWS, (i + block) * ROWS)
            for n, h in enumerate(halves):
                part[kind, j, h, there, :] += term[:, n * LANES : (n + 1) * LANES]

    def group(t, j, kind):
        zpart[...] = mix(t, j, kind)
        update(t, j, kind, zpart, (0, 1))

    def edges(t, j, send_on):
        @pl.when(has_left)
        def _():
            to_right(t, j).wait_recv()

            @pl.when(t > 0)
            def _():
                to_left(t, j).wait_send()

        @pl.when(has_right)
        def _():
            to_left(t, j).wait_recv()

            @pl.when(t > 0)
            def _():
                to_right(t, j).wait_send()

        group(t, j, OUTER)
        send_on(j)

    def send_whole(t, j):
        @pl.when(has_left)
        def _():
            to_left(t, j).start()

        @pl.when(has_right)
        def _():
            to_right(t, j).start()

    def half_to(side, h, j):
        b = (ITERS - 1) % 2
        rows = pl.ds(PAD + j * ROWS, ROWS)
        deep = pl.ds(h * LANES, LANES)
        here, there = ((4, NX + 4), (NX, 0))[side]
        return pltpu.make_async_remote_copy(
            src_ref=wave.at[b, pl.ds(here, 4), rows, deep],
            dst_ref=wave.at[b, pl.ds(there, 4), rows, deep],
            send_sem=send.at[side, ITERS - 1 + h, j],
            recv_sem=recv.at[side, ITERS - 1 + h, j],
            device_id=(left, right)[side],
            device_id_type=MESH,
        )

    def send_half(h, j):
        @pl.when(has_left)
        def _():
            half_to(0, h, j).start()

        @pl.when(has_right)
        def _():
            half_to(1, h, j).start()

    def last_edges(h, j):
        if h == 0:
            zlast[j] = mix(ITERS - 1, j, OUTER)

        @pl.when(has_left)
        def _():
            half_to(1, h, j).wait_recv()

        @pl.when(has_right)
        def _():
            half_to(0, h, j).wait_recv()

        update(ITERS - 1, j, OUTER, zlast.at[j], (h,))

    def last_copy(j):
        rows = pl.ds(pl.multiple_of(PAD + j * ROWS, 8), ROWS)
        plain = pl.ds(pl.multiple_of(j * ROWS, ROWS), ROWS)
        return pltpu.make_async_copy(wave.at[ITERS % 2, pl.ds(4, NX), rows], last.at[0, :, plain], store.at[j])

    prior_copy = pltpu.make_async_copy(wave.at[((ITERS + 1) % 2, *inner)], prior.at[0], store.at[CHUNKS])

    def give(j, half=None):
        index = (INNER, j) if half is None else (OUTER, j, half)
        which = 0 if half is None else 1 + half
        return pltpu.make_async_remote_copy(
            src_ref=part.at[index],
            dst_ref=other.at[index],
            send_sem=swap.at[0, which, j],
            recv_sem=swap.at[1, which, j],
            device_id=partner,
            device_id_type=MESH,
        )

    row_at = grid((1024, 1), 0)
    slot_row = f32(row_at // 256 * 512 + lax.rem(row_at, 256))
    lane = grid((1, LANES), 1)

    def fold(pair, half=None):
        kind, halves = (INNER, (0, 1)) if half is None else (OUTER, (half,))
        for j in (2 * pair, 2 * pair + 1):
            give(j, half).wait_recv()
        for h in halves:
            for r in range(BY):
                both = jnp.concatenate(
                    [ref[kind, 2 * pair + j, h, pl.ds(r, HELD, stride=BY), :] for ref in (part, other) for j in (0, 1)], axis=0
                )
                hi = bf(both)
                there = slice(r % 2 * LANES, (r % 2 + 1) * LANES)
                rhs[h, r // 2, 0:LANES, there] = hi
                rhs[h, r // 2, LANES : 2 * LANES, there] = bf(both - f32(hi))
        row = pl.ds(kind * FOLDS + pair, 1)
        named = jnp.where(lane < PAIR, keys[row, :], other_keys[row, :])
        named = jnp.concatenate([named, named], axis=1)

        def tiles(i, _):
            first = i * 4
            pick = bf(f32(named - f32(first * 512 + core * 256) == slot_row))
            for h in halves:
                for r in range(0, BY, 2):
                    sums = jnp.dot(pick, rhs[h, r // 2], preferred_element_type=jnp.float32)
                    for n in range(2):
                        dense[h * BY + r + n, pl.ds(first, 4)] += sums[:, n * LANES : (n + 1) * LANES].reshape(4, 4, 4, TSLOTS, LANES)
            return 0

        lax.fori_loop(0, 1, tiles, 0)

    def each(body):
        lax.fori_loop(0, CHUNKS, lambda j, _: (body(j), 0)[1], 0)

    each(lambda j: group(0, j, INNER))

    def one_step(t, _):
        for s in range(ITERS - 2):

            @pl.when(t == s)
            def _():
                loads[4 + s].wait()

        def one_chunk(j):
            edges(t, j, lambda j: send_whole(t + 1, j))

            @pl.when(j > 0)
            def _():
                group(t + 1, j - 1, INNER)

        each(one_chunk)
        group(t + 1, CHUNKS - 1, INNER)
        return 0

    lax.fori_loop(0, ITERS - 2, one_step, 0)
    loads[2 + ITERS].wait()
    key_swap.wait_recv()

    def third_chunk(j):
        edges(ITERS - 2, j, lambda j: send_half(0, j))

        @pl.when(j > 0)
        def _():
            group(ITERS - 1, j - 1, INNER)
            give(j - 1).start()

        @pl.when(jnp.logical_and(j >= 3, lax.rem(j, 2) == 1))
        def _():
            fold((j - 3) // 2)

    each(third_chunk)
    prior_copy.start()
    group(ITERS - 1, CHUNKS - 1, INNER)
    give(CHUNKS - 1).start()

    def last_chunk(h, j):
        if h == 0:
            send_half(1, j)
        last_edges(h, j)
        give(j, h).start()
        if h == 0:

            @pl.when(j == 1)
            def _():
                fold(FOLDS - 1)

        else:
            last_copy(j).start()

        @pl.when(jnp.logical_and(j >= 3, lax.rem(j, 2) == 1))
        def _():
            fold((j - 3) // 2, h)

    def toward(p, stage, by):
        return lax.rem(place[PARTS[p][2][stage]] + by, 4)

    def block(p, stage, dest, half=None):
        tile, tiles, order = PARTS[p]
        index = [slice(None)] * 3
        for axis in order[:stage]:
            index[axis] = place[axis]
        index[order[stage]] = dest
        if half is not None:
            index[order[stage + 1]] = pl.ds(2 * half, 2)
        return (pl.ds(tile, tiles), *index)

    def message(p, kind):
        by = 1 if kind < 3 else 3
        return pltpu.make_async_remote_copy(
            src_ref=dense.at[block(p, 0, toward(p, 0, 2 if kind % 3 == 0 else by), 0 if kind in (0, 2, 4) else 1)],
            dst_ref=ring[p].at[kind],
            send_sem=post.at[p, kind],
            recv_sem=mail.at[p, kind],
            device_id=beside(PARTS[p][2][0], by),
            device_id_type=MESH,
        )

    def straight(p, stage, by):
        return pltpu.make_async_remote_copy(
            src_ref=dense.at[block(p, stage, toward(p, stage, by))],
            dst_ref=(direct, final)[stage - 1][p].at[by - 1],
            send_sem=post.at[p, 3 + 3 * stage + by - 1],
            recv_sem=mail.at[p, 3 + 3 * stage + by - 1],
            device_id=beside(PARTS[p][2][stage], by),
            device_id_type=MESH,
        )

    def add(where, *terms):
        total = dense[where]
        for term in terms:
            total = total + term
        dense[where] = total

    def far(p):
        message(p, 0).start()
        message(p, 3).start()

    def near(p):
        message(p, 1).start()
        message(p, 4).start()

    def merged(p):
        message(p, 0).wait_recv()
        add(block(p, 0, toward(p, 0, 1), 0), ring[p][0])
        message(p, 2).start()
        message(p, 3).wait_recv()
        add(block(p, 0, toward(p, 0, 3), 1), ring[p][3])
        message(p, 5).start()

    def second(p):
        for kind in (1, 4, 2, 5):
            message(p, kind).wait_recv()
        add(block(p, 0, toward(p, 0, 0), 0), ring[p][2], ring[p][4])
        add(block(p, 0, toward(p, 0, 0), 1), ring[p][1], ring[p][5])
        for by in (2, 1, 3):
            straight(p, 1, by).start()

    def third(p):
        for by in (2, 1, 3):
            straight(p, 1, by).wait_recv()
        add(block(p, 1, toward(p, 1, 0)), direct[p][0], direct[p][1], direct[p][2])
        for by in (2, 1, 3):
            straight(p, 2, by).start()

    def done(p):
        for by in (2, 1, 3):
            straight(p, 2, by).wait_recv()
        tile, tiles, _ = PARTS[p]
        for i in range(tiles):
            total = dense[(tile + i, *place)] + final[p][0, i] + final[p][1, i] + final[p][2, i]
            first_lane = ((tile + i) % BY * HALVES + (tile + i) // BY) * LANES
            out[0, :, first_lane : first_lane + LANES] = total

    def carry_out(*plan):
        for action, parts in plan:
            for p in parts:
                action(p)

    each(functools.partial(last_chunk, 0))
    fold(FOLDS - 1, 0)
    carry_out((far, EARLY), (near, EARLY))
    each(functools.partial(last_chunk, 1))
    carry_out((merged, EARLY))
    fold(FOLDS - 1, 1)
    carry_out((far, LATE), (near, LATE), (second, EARLY), (merged, LATE), (second, LATE))
    carry_out((third, EARLY), (third, LATE), (done, EARLY), (done, LATE))

    for p in range(count_parts):
        for kind in range(6):
            message(p, kind).wait_send()
        for stage in (1, 2):
            for by in (1, 2, 3):
                straight(p, stage, by).wait_send()

    def finish(j):
        last_copy(j).wait()
        for half in (None, 0, 1):
            give(j, half).wait_send()
        rows = pl.ds(j * ROWS, ROWS)

        @pl.when(has_left)
        def _():
            to_left(0, j, now.at[0, pl.ds(0, 4), rows]).wait_send()
            for h in range(HALVES):
                half_to(0, h, j).wait_send()

        @pl.when(has_right)
        def _():
            to_right(0, j, now.at[0, pl.ds(NX - 4, 4), rows]).wait_send()
            for h in range(HALVES):
                half_to(1, h, j).wait_send()

    each(finish)
    key_swap.wait_send()
    prior_copy.wait()


def run(now, before, courant, source, tiles_here, slots_here):
    field = pltpu.VMEM((1, NX, CY, CZ), jnp.float32)
    ring, direct, final = [], [], []
    for _, tiles, order in PARTS:
        sizes = [2 if axis == order[1] else 4 for axis in range(3) if axis != order[0]]
        ring.append(pltpu.VMEM((6, tiles, *sizes, TSLOTS, LANES), jnp.float32))
        direct.append(pltpu.VMEM((3, tiles, 4, TSLOTS, LANES), jnp.float32))
        final.append(pltpu.VMEM((3, tiles, TSLOTS, LANES), jnp.float32))
    return pl.pallas_call(
        kernel,
        out_shape=(field, field, pltpu.VMEM((1, TSLOTS, BY * CZ), jnp.float32)),
        in_specs=[pl.BlockSpec(memory_space=pl.ANY)] * 4 + [pl.BlockSpec(memory_space=pltpu.VMEM)] * 2,
        out_specs=(pl.BlockSpec(memory_space=pltpu.VMEM),) * 3,
        scratch_shapes=[
            pltpu.VMEM((2, NX + 8, CY + 2 * PAD, CZ), jnp.float32),
            pltpu.VMEM((NX, CY, CZ), jnp.float32),
            pltpu.VMEM((ITERS, NX, CY, CZ), jnp.bfloat16),
            pltpu.VMEM((2, CHUNKS, HALVES, GROUP * ROWS, LANES), jnp.float32),
            pltpu.VMEM((2, CHUNKS, HALVES, GROUP * ROWS, LANES), jnp.float32),
            pltpu.VMEM((GROUP, ROWS, CZ), jnp.float32),
            pltpu.VMEM((CHUNKS, GROUP, ROWS, CZ), jnp.float32),
            pltpu.VMEM((CZ, CZ), jnp.bfloat16),
            pltpu.VMEM((GROUP * ROWS, GROUP * WIDE), jnp.bfloat16),
            pltpu.VMEM((2 * FOLDS, LANES), jnp.float32),
            pltpu.VMEM((2 * FOLDS, LANES), jnp.float32),
            pltpu.VMEM((HALVES, BY // 2, 4 * PAIR, 2 * LANES), jnp.bfloat16),
            pltpu.VMEM((BY * HALVES, 4, 4, 4, TSLOTS, LANES), jnp.float32),
            *ring,
            *direct,
            *final,
            pltpu.SemaphoreType.DMA((3 + ITERS,)),
            pltpu.SemaphoreType.DMA((2, ITERS + 1, CHUNKS)),
            pltpu.SemaphoreType.DMA((2, ITERS + 1, CHUNKS)),
            pltpu.SemaphoreType.DMA((CHUNKS + 1,)),
            pltpu.SemaphoreType.DMA((2, 3, CHUNKS)),
            pltpu.SemaphoreType.DMA((2,)),
            pltpu.SemaphoreType.DMA((len(PARTS), 12)),
            pltpu.SemaphoreType.DMA((len(PARTS), 12)),
        ],
        compiler_params=pltpu.CompilerParams(collective_id=0, has_side_effects=True, vmem_limit_bytes=59 * MIB),
        cost_estimate=pl.CostEstimate(flops=5_000_000_000, bytes_accessed=16_000_000, transcendentals=0),
    )(now, before, courant, source, tiles_here, slots_here)


def keep(*refs):
    semaphores = refs[6]
    copies = [pltpu.make_async_copy(refs[i], refs[3 + i], semaphores.at[i]) for i in range(3)]
    for copy in copies:
        copy.start()
    for copy in copies:
        copy.wait()


def on_device(wave_now, wave_before, courant, source_waves, tile_ids, slot_ids):
    results = run(wave_now, wave_before, courant, source_waves, tile_ids.reshape(1, NBLK), slot_ids.reshape(1, NBLK))
    return pl.pallas_call(
        keep,
        out_shape=tuple(jax.ShapeDtypeStruct(v.shape, v.dtype) for v in results),
        in_specs=[pl.BlockSpec(memory_space=pl.ANY)] * 3,
        out_specs=(pl.BlockSpec(memory_space=pl.ANY),) * 3,
        scratch_shapes=[pltpu.SemaphoreType.DMA((3,))],
        compiler_params=pltpu.CompilerParams(vmem_limit_bytes=MIB),
    )(*results)


def solution(mesh):
    return jax.shard_map(
        on_device,
        mesh=mesh,
        in_specs=(
            P("shot", "sub"),
            P("shot", "sub"),
            P("shot", "sub"),
            P(None, "shot", "sub"),
            P("shot", "sub", None),
            P("shot", "sub"),
        ),
        out_specs=(
            P("shot", "sub"),
            P("shot", "sub"),
            P(("shot", "sub")),
        ),
        check_vma=False,
    )
```

time: 90.8 us -> 85.9 us (0.946)
  Pallas kernels: 89.6 us -> 85.1 us
    pallas_call x1, Pallas kernels: 87.6 us -> 83 us  [run(): pl.pallas_call(kernel, out_shape=(field, field, pltpu.VMEM((1, TSLOTS, BY...]
where the time goes in v3:
time: 85.9 us; the launch traced here: 85.7 us
  Pallas kernels  85.1 us (99%)
    pallas_call x1, Pallas kernels, run(): pl.pallas_call(kernel, out_shape=(field, field, pltpu.VMEM((1, TSLOTS, BY...  83 us
    pallas_call x1, Pallas kernels, on_device(): pl.pallas_call(keep, out_shape=tuple((jax.ShapeDtypeStruct(v.shape, v.dty...  2.04 us

profile of v3, /device:TPU:0, one launch (start us, length us, event | category | flops | bytes accessed | tf_op | source)
XLA Modules:
  0.0 85.7 jit_solution(3783401627245258151)
XLA Ops:
  0.6 83.0 %shard_map.85 = (f32[1,16,128,256]{3,2,1,0:T(8,128)S(1)}, f32[1,16,128,256]{3,2,1,0:T(8,128)S(1)}, f32[1,16,1024]{2,1,0:T(8,128)S(1)}) custom-call(f32[1,16,128,256]{3,2,1,0:T(8,128)} %now.1, f32[1,16,128,256]{3,2,1,0:T(8,128)} %before.1, f32[1,16,128,256]{3,2,1,0:T(8,128)} %courant.1, bf16[4,1,16,128,256]{4,3,2,1,0:T(8,128)(2,1)} %source.1, ...), custom_call_target="tpu_custom_call" | custom-call | flops 5000000000 | bytes 16000000 | tf_op jit(solution)/shard_map/pallas_call | solution.py:537
  83.7 2.0 %shard_map.86 = (f32[1,16,128,256]{3,2,1,0:T(8,128)}, f32[1,16,128,256]{3,2,1,0:T(8,128)}, f32[1,16,1024]{2,1,0:T(8,128)}) custom-call(f32[1,16,128,256]{3,2,1,0:T(8,128)S(1)} %get-tuple-element.6.refs_0_, f32[1,16,128,256]{3,2,1,0:T(8,128)S(1)} %get-tuple-element.7.refs_1_, f32[1,16,1024]{2,1,0:T(8,128)S(1)} %get-tuple-element.8.refs_2_), custom_call_target="tpu_custom_call" | custom-call | tf_op jit(solution)/shard_map/pallas_call | solution.py:584

commit v4 on v3

--- a/solution.py
+++ b/solution.py
@@ -38,6 +38,7 @@
     (7, 1, (1, 0, 2)),
 )
 EARLY, LATE = (0, 1), (2, 3, 4, 5)
+ALONG, OTHERS = (2, 3), (4, 5)
 
 
 def bf(v):
@@ -340,8 +341,8 @@
 
         lax.fori_loop(0, 1, tiles, 0)
 
-    def each(body):
-        lax.fori_loop(0, CHUNKS, lambda j, _: (body(j), 0)[1], 0)
+    def each(body, first=0, end=CHUNKS):
+        lax.fori_loop(first, end, lambda j, _: (body(j), 0)[1], 0)
 
     each(lambda j: group(0, j, INNER))
 
@@ -489,12 +490,21 @@
 
     each(functools.partial(last_chunk, 0))
     fold(FOLDS - 1, 0)
-    carry_out((far, EARLY), (near, EARLY))
-    each(functools.partial(last_chunk, 1))
+    carry_out((far, EARLY))
+    each(functools.partial(last_chunk, 1), 0, 2)
+    carry_out((near, EARLY))
+    each(functools.partial(last_chunk, 1), 2, 8)
     carry_out((merged, EARLY))
     fold(FOLDS - 1, 1)
-    carry_out((far, LATE), (near, LATE), (second, EARLY), (merged, LATE), (second, LATE))
-    carry_out((third, EARLY), (third, LATE), (done, EARLY), (done, LATE))
+    carry_out((far, LATE))
+    carry_out((near, LATE))
+    carry_out((second, EARLY))
+    carry_out((merged, LATE))
+    carry_out((third, EARLY))
+    carry_out((second, LATE))
+    carry_out((done, EARLY))
+    carry_out((third, LATE))
+    carry_out((done, LATE))
 
     for p in range(count_parts):
         for kind in range(6):

time: 85.9 us -> 85.5 us (level)
  no operation moved by 1% of the time
where the time goes in v4:
time: 85.5 us; the launch traced here: 85.4 us
  Pallas kernels  84.8 us (99%)
    pallas_call x1, Pallas kernels, run(): pl.pallas_call(kernel, out_shape=(field, field, pltpu.VMEM((1, TSLOTS, BY...  82.7 us
    pallas_call x1, Pallas kernels, on_device(): pl.pallas_call(keep, out_shape=tuple((jax.ShapeDtypeStruct(v.shape, v.dty...  2.04 us

profile of v4, /device:TPU:0, one launch (start us, length us, event | category | flops | bytes accessed | tf_op | source)
XLA Modules:
  0.0 85.4 jit_solution(4271301521881861342)
XLA Ops:
  0.6 82.7 %shard_map.85 = (f32[1,16,128,256]{3,2,1,0:T(8,128)S(1)}, f32[1,16,128,256]{3,2,1,0:T(8,128)S(1)}, f32[1,16,1024]{2,1,0:T(8,128)S(1)}) custom-call(f32[1,16,128,256]{3,2,1,0:T(8,128)} %now.1, f32[1,16,128,256]{3,2,1,0:T(8,128)} %before.1, f32[1,16,128,256]{3,2,1,0:T(8,128)} %courant.1, bf16[4,1,16,128,256]{4,3,2,1,0:T(8,128)(2,1)} %source.1, ...), custom_call_target="tpu_custom_call" | custom-call | flops 5000000000 | bytes 16000000 | tf_op jit(solution)/shard_map/pallas_call | solution.py:547
  83.4 2.0 %shard_map.86 = (f32[1,16,128,256]{3,2,1,0:T(8,128)}, f32[1,16,128,256]{3,2,1,0:T(8,128)}, f32[1,16,1024]{2,1,0:T(8,128)}) custom-call(f32[1,16,128,256]{3,2,1,0:T(8,128)S(1)} %get-tuple-element.6.refs_0_, f32[1,16,128,256]{3,2,1,0:T(8,128)S(1)} %get-tuple-element.7.refs_1_, f32[1,16,1024]{2,1,0:T(8,128)S(1)} %get-tuple-element.8.refs_2_), custom_call_target="tpu_custom_call" | custom-call | tf_op jit(solution)/shard_map/pallas_call | solution.py:594

commit v5 on v3

--- a/solution.py
+++ b/solution.py
@@ -38,6 +38,7 @@
     (7, 1, (1, 0, 2)),
 )
 EARLY, LATE = (0, 1), (2, 3, 4, 5)
+ALONG, OTHERS = (2, 3), (4, 5)
 
 
 def bf(v):
@@ -340,8 +341,8 @@
 
         lax.fori_loop(0, 1, tiles, 0)
 
-    def each(body):
-        lax.fori_loop(0, CHUNKS, lambda j, _: (body(j), 0)[1], 0)
+    def each(body, first=0, end=CHUNKS):
+        lax.fori_loop(first, end, lambda j, _: (body(j), 0)[1], 0)
 
     each(lambda j: group(0, j, INNER))
 
@@ -489,19 +490,14 @@
 
     each(functools.partial(last_chunk, 0))
     fold(FOLDS - 1, 0)
-    carry_out((far, EARLY), (near, EARLY))
-    each(functools.partial(last_chunk, 1))
-    carry_out((merged, EARLY))
-    fold(FOLDS - 1, 1)
-    carry_out((far, LATE), (near, LATE), (second, EARLY), (merged, LATE), (second, LATE))
-    carry_out((third, EARLY), (third, LATE), (done, EARLY), (done, LATE))
-
-    for p in range(count_parts):
+    def sent(p, stage):
+        for by in (1, 2, 3):
+            straight(p, stage, by).wait_send()
+
+    def sent_ring(p):
         for kind in range(6):
             message(p, kind).wait_send()
-        for stage in (1, 2):
-            for by in (1, 2, 3):
-                straight(p, stage, by).wait_send()
+        sent(p, 1)
 
     def finish(j):
         last_copy(j).wait()
@@ -521,9 +517,29 @@
             for h in range(HALVES):
                 half_to(1, h, j).wait_send()
 
+    carry_out((far, EARLY))
+    each(functools.partial(last_chunk, 1), 0, 2)
+    carry_out((near, EARLY))
+    each(functools.partial(last_chunk, 1), 2, 8)
+    carry_out((merged, EARLY))
+    fold(FOLDS - 1, 1)
+    carry_out((far, LATE))
+    carry_out((near, LATE))
     each(finish)
     key_swap.wait_send()
     prior_copy.wait()
+    carry_out((second, EARLY))
+    carry_out((merged, LATE))
+    carry_out((third, EARLY))
+    carry_out((second, LATE))
+    carry_out((sent_ring, EARLY))
+    carry_out((done, EARLY))
+    carry_out((third, LATE))
+    carry_out((sent_ring, LATE))
+    carry_out((done, LATE))
+
+    for p in range(count_parts):
+        sent(p, 2)
 
 
 def run(now, before, courant, source, tiles_here, slots_here):

time: 85.9 us -> 85.3 us (level)
  no operation moved by 1% of the time
where the time goes in v5:
time: 85.3 us; the launch traced here: 85.2 us
  Pallas kernels  84.6 us (99%)
    pallas_call x1, Pallas kernels, run(): pl.pallas_call(kernel, out_shape=(field, field, pltpu.VMEM((1, TSLOTS, BY...  82.5 us
    pallas_call x1, Pallas kernels, on_device(): pl.pallas_call(keep, out_shape=tuple((jax.ShapeDtypeStruct(v.shape, v.dty...  2.04 us

profile of v5, /device:TPU:0, one launch (start us, length us, event | category | flops | bytes accessed | tf_op | source)
XLA Modules:
  0.0 85.2 jit_solution(10962220496276046946)
XLA Ops:
  0.6 82.5 %shard_map.85 = (f32[1,16,128,256]{3,2,1,0:T(8,128)S(1)}, f32[1,16,128,256]{3,2,1,0:T(8,128)S(1)}, f32[1,16,1024]{2,1,0:T(8,128)S(1)}) custom-call(f32[1,16,128,256]{3,2,1,0:T(8,128)} %now.1, f32[1,16,128,256]{3,2,1,0:T(8,128)} %before.1, f32[1,16,128,256]{3,2,1,0:T(8,128)} %courant.1, bf16[4,1,16,128,256]{4,3,2,1,0:T(8,128)(2,1)} %source.1, ...), custom_call_target="tpu_custom_call" | custom-call | flops 5000000000 | bytes 16000000 | tf_op jit(solution)/shard_map/pallas_call | solution.py:553
  83.2 2.0 %shard_map.86 = (f32[1,16,128,256]{3,2,1,0:T(8,128)}, f32[1,16,128,256]{3,2,1,0:T(8,128)}, f32[1,16,1024]{2,1,0:T(8,128)}) custom-call(f32[1,16,128,256]{3,2,1,0:T(8,128)S(1)} %get-tuple-element.6.refs_0_, f32[1,16,128,256]{3,2,1,0:T(8,128)S(1)} %get-tuple-element.7.refs_1_, f32[1,16,1024]{2,1,0:T(8,128)S(1)} %get-tuple-element.8.refs_2_), custom_call_target="tpu_custom_call" | custom-call | tf_op jit(solution)/shard_map/pallas_call | solution.py:600
